TPU v7x, 128 devices: a whole 4x4x4 slice. The times are simulated.
128 devices in a mesh: clip: 64 (over x, z, y_lo, core), space: 2 (over y_hi).
Axes of the slice: x: 4, y: 4 (y_hi: 2, y_lo: 2; y = y_hi * 2 + y_lo), z: 4, core: 2. Of those that a mesh axis runs over, the one named last changes fastest.
Arguments:
- latent: bfloat16 [1024, 96, 1280], P('clip', 'space'), may hold values from -160 to 160
- gn_gain: float32 [1280], replicated, may hold values from 0.1 to 1.9
- gn_bias: float32 [1280], replicated, may hold values from -3 to 3
- w_query: bfloat16 [1280, 1280], replicated, may hold values from -2 to 2
- w_key: bfloat16 [1280, 1280], replicated, may hold values from -2 to 2
- w_value: bfloat16 [1280, 1280], replicated, may hold values from -0.15625 to 0.15625
- w_out: bfloat16 [1280, 1280], replicated, may hold values from -0.15625 to 0.15625
- out_bias: float32 [1280], replicated, may hold values from -3 to 3
- context_frames: int32 [64, 1], P('clip'), may hold values from 0 to 15
Outputs:
- mixed: bfloat16 [1024, 96, 1280], P('clip', 'space')
All inputs are finite; a program needn't handle non-finite values.
Results may differ from a plain program's by a relative error of at most 0.0034.
The roundings to bfloat16 on the way count: a program that leaves them out, or rounds other values in their place, can miss the bound.
Values may be sent and summed in bfloat16 or wider, within the bound.
A program may use at most 192 MiB of HBM per device.

v0:
```python
import math

import jax
import jax.numpy as jnp
from jax import lax
from jax.sharding import PartitionSpec as P

HEAD_DIM = 64
GROUPS = 32
EDGE = 4


EPS = 1e-06


def with_halo(cells, sides, width):
    for axis, dim in sides:
        count = lax.axis_size(axis)
        ends = count - 1
        head = lax.slice_in_dim(cells, 0, width, axis=dim)
        tail = lax.slice_in_dim(cells, cells.shape[dim] - width, cells.shape[dim], axis=dim)
        cells = jnp.concatenate(
            [
                lax.ppermute(tail, axis, [(i, (i + 1) % count) for i in range(ends)]),
                cells,
                lax.ppermute(head, axis, [((i + 1) % count, i) for i in range(ends)]),
            ],
            axis=dim,
        )
    return cells


def project(rows_in, weight):
    flat = rows_in.reshape(-1, rows_in.shape[-1])
    out = jnp.dot(flat, weight, preferred_element_type=jnp.float32).astype(jnp.bfloat16)
    return out.reshape(rows_in.shape[:-1] + (weight.shape[1],))


def local(latent, gn_gain, gn_bias, w_query, w_key, w_value, w_out, out_bias, context_frames):
    frames, rows, width = latent.shape
    per = width // GROUPS
    x = latent.astype(jnp.float32).reshape(frames, rows, GROUPS, per)
    count = frames * rows * lax.axis_size("space") * per
    mean = lax.psum(jnp.sum(x, axis=(0, 1, 3)), "space") / count
    centred = x - mean[:, None]
    var = lax.psum(jnp.sum(centred * centred, axis=(0, 1, 3)), "space") / count
    normed = (centred * lax.rsqrt(var + EPS)[:, None]).reshape(frames, rows, width)
    normed = (normed * gn_gain + gn_bias).astype(jnp.bfloat16)
    query = project(normed, w_query)
    stacked = jnp.stack([project(normed, w_key), project(normed, w_value)])
    padded = with_halo(stacked, (("clip", 1),), EDGE)
    picks = context_frames[0]
    remote = lax.all_gather(jnp.take(stacked, picks, axis=1), "clip", axis=1, tiled=True)
    gathered = jnp.concatenate([padded, remote], axis=1)
    count_keys = gathered.shape[1]
    clip_place = lax.axis_index("clip")
    valid = jnp.concatenate(
        [
            jnp.full((EDGE,), clip_place > 0),
            jnp.ones((frames,), bool),
            jnp.full((EDGE,), clip_place < lax.axis_size("clip") - 1),
            jnp.ones((remote.shape[1],), bool),
        ]
    )
    heads = width // HEAD_DIM
    q_heads = query.reshape(frames, rows, heads, HEAD_DIM)
    k_heads = gathered[0].reshape(count_keys, rows, heads, HEAD_DIM)
    v_heads = gathered[1].reshape(count_keys, rows, heads, HEAD_DIM)
    scores = jnp.einsum("fphd,kphd->phfk", q_heads, k_heads, preferred_element_type=jnp.float32) * (
        1.0 / math.sqrt(HEAD_DIM)
    )
    scores = jnp.where(valid[None, None, None, :], scores, -jnp.inf)
    top = jnp.max(scores, axis=-1, keepdims=True)
    expo = jnp.exp(scores - top)
    weights = (expo / jnp.sum(expo, axis=-1, keepdims=True)).astype(jnp.bfloat16)
    attended = jnp.einsum("phfk,kphd->fphd", weights, v_heads, preferred_element_type=jnp.float32)
    attended = attended.reshape(frames * rows, width).astype(jnp.bfloat16)
    branch = jnp.dot(attended, w_out, preferred_element_type=jnp.float32).reshape(
        frames, rows, width
    )
    return (latent.astype(jnp.float32) + branch + out_bias).astype(jnp.bfloat16)


def solution(mesh):
    placed = (P("clip", "space", None), P(), P(), P(), P(), P(), P(), P(), P("clip", None))
    return jax.shard_map(
        local, mesh=mesh, in_specs=placed, out_specs=P("clip", "space", None), check_vma=False
    )
```

profile of v0, /device:TPU:1, one launch (start us, length us, event | category | flops | bytes accessed | tf_op | source)
XLA Modules:
  0.0 279.9 jit_solution(2569508072030211423)
XLA Ops:
  7.4 2.0 convert_reduce_fusion
  9.4 0.1 reduce_sum.32
  9.5 0.1 reduce_sum.36
  9.6 6.1 %psum.14 = f32[32]{0:T(128)S(1)} all-reduce(f32[32]{0:T(128)S(1)} %reduce_sum.36), channel_id=1, replica_groups=mesh['clip'=64,'space'=2] {'space'}, use_global_device_ids=true, to_apply=%region_2.0 | all-reduce | flops 32 | bytes 256 | tf_op jit(solution)/shard_map/psum | solution.py:44
  15.7 0.1 sub.23
  15.8 2.1 fusion.4
  17.9 0.1 reduce_sum.45
  18.0 0.1 reduce_sum.46
  18.1 5.3 %psum.15 = f32[32]{0:T(128)S(1)} all-reduce(f32[32]{0:T(128)S(1)} %reduce_sum.46), channel_id=1, replica_groups=mesh['clip'=64,'space'=2] {'space'}, use_global_device_ids=true, to_apply=%region_5.6 | all-reduce | flops 32 | bytes 256 | tf_op jit(solution)/shard_map/psum | solution.py:46
  23.5 0.1 mul.33
  23.6 2.3 fusion.7
  25.9 2.7 convolution_convert_fusion.2
  28.7 2.7 convolution_convert_fusion.1
  31.4 0.8 fusion.21
  32.3 2.5 fusion.18
  34.8 6.1 %collective-permute-start = (bf16[2,4,48,1280]{3,2,1,0:T(8,128)(2,1)}, bf16[2,4,48,1280]{3,2,1,0:T(8,128)(2,1)}, u32[]{:S(2)}, u32[]{:S(2)}) collective-permute-start(bf16[2,4,48,1280]{3,2,1,0:T(8,128)(2,1)} %get-tuple-element.18), channel_id=1, source_target_pairs={{0,2},{2,4},{4,6},{6,8},{8,10},{10,12},{12,14},{14,16},{16,18},{18... | collective-permute-start | bytes 2949128 | tf_op jit(solution)/shard_map/ppermute | solution.py:24
  41.0 2.1 collective-permute-start.1
  43.1 3.9 %convolution_convert_fusion = bf16[768,1280]{1,0:T(8,128)(2,1)} fusion(bf16[768,1280]{1,0:T(8,128)(2,1)S(1)} %bitcast.35, bf16[1280,1280]{1,0:T(8,128)(2,1)S(1)} %copy-done.10), kind=kOutput, calls=%fused_computation.31 | convolution fusion | flops 2517565440 | bytes 7208960 | tf_op jit(solution)/shard_map/dot_general | solution.py:35
  47.0 6.8 %reshape_reshape.3 = bf16[16,48,20,64]{3,2,1,0:T(8,128)(2,1)} reshape(bf16[768,1280]{1,0:T(8,128)(2,1)} %convolution_convert_fusion) | data formatting | bytes 3932160 | tf_op jit(solution)/shard_map/reshape;reshape | solution.py:66
  53.9 0.7 collective-permute-done
  54.6 10.2 %collective-permute-done.1 = bf16[2,4,48,1280]{3,2,1,0:T(8,128)(2,1)} collective-permute-done((bf16[2,4,48,1280]{3,2,1,0:T(8,128)(2,1)S(1)}, bf16[2,4,48,1280]{3,2,1,0:T(8,128)(2,1)}, u32[]{:S(2)}, u32[]{:S(2)}) %collective-permute-start.1) | collective-permute-done | bytes 983072 | tf_op jit(solution)/shard_map/ppermute | solution.py:26
  64.8 105.5 %all-gather.2.cloned.1.call-done = bf16[2,64,48,1280]{3,2,1,0:T(8,128)(2,1)} async-done(((bf16[2,1,48,1280]{3,2,1,0:T(8,128)(2,1)}), bf16[2,64,48,1280]{3,2,1,0:T(8,128)(2,1)}) %all-gather.2.cloned.1.call-update) | async-done | bytes 15728656 | tf_op jit(solution)/shard_map/all_gather | solution.py:53
  170.3 9.6 %pad_maximum_fusion = bf16[2,88,48,1280]{3,2,1,0:T(8,128)(2,1)S(1)} fusion(bf16[2,64,48,1280]{3,2,1,0:T(8,128)(2,1)} %all-gather.2.cloned.1.call-done, bf16[2,4,48,1280]{3,2,1,0:T(8,128)(2,1)} %collective-permute-done.1, bf16[1,16,48,1280]{3,2,1,0:T(8,128)(2,1)} %bitcast.31, bf16[1,16,48,1280]{3,2,1,0:T(8,128)(2,1)S(1)} %bitcast.28, ...), kind=kLoop, calls=%fused_computation.1 | loop fusion | flops 43253760 | bytes 43253760 | tf_op jit(solution)/shard_map/concatenate | solution.py:54
  179.9 7.7 %fusion.24 = (bf16[1,88,48,1280]{3,2,1,0:T(8,128)(2,1)}, bf16[1,88,48,1280]{3,2,1,0:T(8,128)(2,1)}) fusion(bf16[2,88,48,1280]{3,2,1,0:T(8,128)(2,1)S(1)} %pad_maximum_fusion), kind=kLoop, calls=%fused_computation.44 | loop fusion | bytes 43253760 | tf_op jit(solution)/shard_map/slice | solution.py:67
  187.6 18.7 %copy.18 = bf16[1,88,48,1280]{1,3,2,0:T(8,128)(2,1)} copy(bf16[1,88,48,1280]{3,2,1,0:T(8,128)(2,1)} %get-tuple-element.16) | data formatting | bytes 21626880 | tf_op jit(solution)/shard_map/slice | solution.py:67
  206.3 18.6 %copy.17 = bf16[1,88,48,1280]{1,3,2,0:T(8,128)(2,1)} copy(bf16[1,88,48,1280]{3,2,1,0:T(8,128)(2,1)} %get-tuple-element.17) | data formatting | bytes 21626880 | tf_op jit(solution)/shard_map/slice | solution.py:68
  224.9 9.0 %fusion.11 = f32[48,20,16,88]{3,2,1,0:T(8,128)S(1)} fusion(bf16[88,48,20,64]{0,3,2,1:T(8,128)(2,1)} %bitcast.25, bf16[16,48,20,64]{3,2,1,0:T(8,128)(2,1)} %reshape_reshape.3), kind=kOutput, calls=%fused_computation.24 | convolution fusion | flops 173015040 | bytes 18186240 | tf_op jit(solution)/shard_map/fphd,kphd->phfk/dot_general | solution.py:69
  234.0 5.7 %fusion.25 = (f32[48,20,16]{2,1,0:T(8,128)S(1)}, f32[48,20,16,88]{3,2,1,0:T(8,128)}) fusion(f32[48,20,16,88]{3,2,1,0:T(8,128)S(1)} %fusion.11, pred[88]{0:T(512)(128)(4,1)S(1)} %pad_add_fusion), kind=kOutput, calls=%fused_computation.45 | output fusion | flops 8110167 | bytes 10874968 | tf_op jit(solution)/shard_map/sub | solution.py:74
  239.6 14.3 %convert_bitcast_fusion = bf16[16,48,20,64]{3,0,2,1:T(8,128)(2,1)} fusion(bf16[88,48,20,64]{0,3,2,1:T(8,128)(2,1)} %bitcast.32, f32[48,20,16,88]{3,2,1,0:T(8,128)} %get-tuple-element.21, f32[48,20,16]{2,1,0:T(8,128)S(1)} %get-tuple-element.20), kind=kOutput, calls=%fused_computation.26 | convolution fusion | flops 176701440 | bytes 18247680 | tf_op jit(solution)/shard_map/phfk,kphd->fphd/dot_general | solution.py:76
  253.9 5.4 %copy.20 = bf16[16,48,20,64]{3,2,1,0:T(8,128)(2,1)} copy(bf16[16,48,20,64]{3,0,2,1:T(8,128)(2,1)} %convert_bitcast_fusion) | data formatting | bytes 3932160 | tf_op jit(solution)/shard_map/convert_element_type | solution.py:77
  259.3 6.5 %convert_element_type.40 = bf16[16,48,1280]{2,1,0:T(8,128)(2,1)} reshape(bf16[16,48,20,64]{3,2,1,0:T(8,128)(2,1)} %copy.20) | data formatting | bytes 3932160 | tf_op jit(solution)/shard_map/convert_element_type | solution.py:77
  265.8 7.2 %fusion.9 = bf16[16,48,1280]{2,1,0:T(8,128)(2,1)} fusion(bf16[16,48,1280]{2,1,0:T(8,128)(2,1)} %param.9, bf16[16,48,1280]{2,1,0:T(8,128)(2,1)} %convert_element_type.40, bf16[1280,1280]{1,0:T(8,128)(2,1)} %param.15, f32[1280]{0:T(1024)S(1)} %copy-done.11), kind=kOutput, calls=%fused_computation.22 | convolution fusion | flops 2520514560 | bytes 9180160 | tf_op jit(solution)/shard_map/dot_general | solution.py:78
  (35 shorter events, 0.3 us)
Async XLA Ops:
  6.5 19.4 %copy-start = (bf16[1280,1280]{1,0:T(8,128)(2,1)S(1)}, bf16[1280,1280]{1,0:T(8,128)(2,1)}, u32[]{:S(2)}) copy-start(bf16[1280,1280]{1,0:T(8,128)(2,1)} %param.13) | copy-start | bytes 9830404
  6.5 17.1 %copy-start.8 = (f32[1280]{0:T(1024)S(1)}, f32[1280]{0:T(1024)}, u32[]{:S(2)}) copy-start(f32[1280]{0:T(1024)} %param.10) | copy-start | bytes 15364
  6.5 17.1 %copy-start.7 = (f32[1280]{0:T(1024)S(1)}, f32[1280]{0:T(1024)}, u32[]{:S(2)}) copy-start(f32[1280]{0:T(1024)} %param.11) | copy-start | bytes 15364
  6.5 163.8 %all-gather.2.cloned.1.call-start = ((), (), s32[]{:S(2)}) async-start(), calls=%async_computation | async-start | bytes 15974400 | tf_op jit(solution)/shard_map/all_gather | solution.py:53
  25.9 2.8 copy-start.5
  25.9 2.8 copy-start.9
  28.7 2.7 copy-start.2
  31.4 3.4 %copy-start.4 = (bf16[768,1280]{1,0:T(8,128)(2,1)}, bf16[768,1280]{1,0:T(8,128)(2,1)S(1)}, u32[]{:S(2)}) copy-start(bf16[768,1280]{1,0:T(8,128)(2,1)S(1)} %convolution_convert_fusion.1) | copy-start | bytes 5898244
  32.3 10.8 %copy-start.6 = (bf16[16,48,1280]{2,1,0:T(8,128)(2,1)S(1)}, bf16[16,48,1280]{2,1,0:T(8,128)(2,1)}, u32[]{:S(2)}) copy-start(bf16[16,48,1280]{2,1,0:T(8,128)(2,1)} %copy-done.5) | copy-start | bytes 5898244
  32.3 10.8 %copy-start.10 = (bf16[1280,1280]{1,0:T(8,128)(2,1)S(1)}, bf16[1280,1280]{1,0:T(8,128)(2,1)}, u32[]{:S(2)}) copy-start(bf16[1280,1280]{1,0:T(8,128)(2,1)} %param.12) | copy-start | bytes 9830404
  34.8 19.7 %collective-permute-start = (bf16[2,4,48,1280]{3,2,1,0:T(8,128)(2,1)}, bf16[2,4,48,1280]{3,2,1,0:T(8,128)(2,1)}, u32[]{:S(2)}, u32[]{:S(2)}) collective-permute-start(bf16[2,4,48,1280]{3,2,1,0:T(8,128)(2,1)} %get-tuple-element.18), channel_id=1, source_target_pairs={{0,2},{2,4},{4,6},{6,8},{8,10},{10,12},{12,14},{14,16},{16,18},{18... | collective-permute-start | bytes 2949128 | tf_op jit(solution)/shard_map/ppermute | solution.py:24
  41.0 23.8 %collective-permute-start.1 = (bf16[2,4,48,1280]{3,2,1,0:T(8,128)(2,1)S(1)}, bf16[2,4,48,1280]{3,2,1,0:T(8,128)(2,1)}, u32[]{:S(2)}, u32[]{:S(2)}) collective-permute-start(bf16[2,4,48,1280]{3,2,1,0:T(8,128)(2,1)S(1)} %get-tuple-element.19), channel_id=1, source_target_pairs={{2,0},{4,2},{6,4},{8,6},{10,8},{12,10},{14,12},{16,14},{18,16},{20... | collective-permute-start | bytes 2949128 | tf_op jit(solution)/shard_map/ppermute | solution.py:26
  47.0 123.4 %copy-start.3 = (bf16[768,1280]{1,0:T(8,128)(2,1)S(1)}, bf16[768,1280]{1,0:T(8,128)(2,1)}, u32[]{:S(2)}) copy-start(bf16[768,1280]{1,0:T(8,128)(2,1)} %copy-done.2) | copy-start | bytes 5898244
  259.3 6.5 %copy-start.11 = (f32[1280]{0:T(1024)S(1)}, f32[1280]{0:T(1024)}, u32[]{:S(2)}) copy-start(f32[1280]{0:T(1024)} %param.16) | copy-start | bytes 15364
  265.8 7.2 %copy-start.1 = (bf16[1280,1280]{1,0:T(8,128)(2,1)S(1)}, bf16[1280,1280]{1,0:T(8,128)(2,1)}, u32[]{:S(2)}) copy-start(bf16[1280,1280]{1,0:T(8,128)(2,1)} %param.13) | copy-start | bytes 9830404
Sparse Core Ops, SparseCore 0:
  32.4 137.8 all-gather.1
where the time goes:
time: 281 us; the launch traced here: 280 us
  waiting for transfers between devices  116 us (41%)
  local copies, waits for them, and re-layouts  64.2 us (23%)
  matrix products  39.9 us (14%)
  other arithmetic  25.3 us (9%)
  between operations  14.4 us (5%)
  blocking collectives  11.4 us (4%)
  starting transfers between devices  8.22 us (3%)
    all_gather x1, waiting for transfers between devices, local(): lax.all_gather(jnp.take(stacked, picks, axis=1), 'clip', axis=1, tiled=True)  106 us
    slice x2, local copies, waits for them, and re-layouts, local(): k_heads = gathered[0].reshape(count_keys, rows, heads, HEAD_DIM)  26.4 us
    slice x1, local copies, waits for them, and re-layouts, local(): v_heads = gathered[1].reshape(count_keys, rows, heads, HEAD_DIM)  18.6 us
    dot_general x1, matrix products, local(): jnp.einsum('phfk,kphd->fphd', weights, v_heads, preferred_element_type=jn...  14.3 us
    convert_element_type x2, local copies, waits for them, and re-layouts, local(): attended = attended.reshape(frames * rows, width).astype(jnp.bfloat16)  11.9 us
    ppermute x1, waiting for transfers between devices, with_halo(): lax.ppermute(head, axis, [((i + 1) % count, i) for i in range(ends)])  10.2 us
    concatenate x1, other arithmetic, local(): gathered = jnp.concatenate([padded, remote], axis=1)  9.58 us
    dot_general x3, matrix products, project(): jnp.dot(flat, weight, preferred_element_type=jnp.float32)  9.31 us
  transfers between devices with their start and end apart: 3, of which 3 were waited for; matrix products, arithmetic and copies ran while one was open for 5% of the time, Pallas kernels for 0%

commit v1 on v0

v1 whole, which is shorter than its diff:
```python
import numpy as np

import jax
import jax.numpy as jnp
from jax import lax
from jax.experimental import pallas as pl
from jax.experimental.pallas import tpu as pltpu
from jax.sharding import PartitionSpec as P

C = 1280
HEAD_DIM = 64
GROUPS = 32
FRAMES = 16
EDGE = 4
EPS = 1e-06
ROWS = 48
HALF = 24
KEYS = 112
TILE = 256
TILES = C // TILE
MESH = pl.DeviceIdType.MESH
F32, BF16 = jnp.float32, jnp.bfloat16


def swap_matrix(outer, inner, blocks=1):
    n = outer * inner
    m = np.zeros((n, n), np.float32)
    for i in range(outer):
        for j in range(inner):
            m[j * outer + i, i * inner + j] = 1
    return m


def edge_merge():
    m = np.zeros((192, 192), np.float32)
    for side in range(2):
        for p in range(HALF):
            for f in range(EDGE):
                m[p * 8 + side * 4 + f, side * 96 + p * 4 + f] = 1
    return m


SWAP16 = swap_matrix(16, 16)
SWAP8 = swap_matrix(16, 8)
EDGE_OUT = swap_matrix(EDGE, ROWS)
EDGE_IN = edge_merge()
GROUP_OF = np.zeros((C, 128), np.float32)
GROUP_OF[np.arange(C), np.arange(C) // (C // GROUPS)] = 1
HEAD_MASK = np.zeros((128, TILE), np.float32)
for _h in range(4):
    HEAD_MASK[_h * 32 : _h * 32 + 32, _h * 64 : _h * 64 + 64] = 1


def dot(a, b):
    return jnp.dot(a, b, preferred_element_type=F32)


def exact_dot(a, b):
    return jnp.dot(a, b, preferred_element_type=F32, precision=lax.Precision.HIGHEST)


def slot_of(i, j, s):
    return j * 8 + i * 2 + s


def kernel(
    latent, gain, shift, wq, wk, wv, wo, out_bias, picks, swap16, swap8, edge_out, edge_in, group_of, group_to, head_mask,
    out,
    lat, normed, turned, sib, ctx, xc, edge_tx, edge_rx, edge_x, query, kv, att, att_tx, result, w, w_out,
    s16, s8, e_out, e_in, g_of, g_to, h_mask, stat_tx, stat_rx, pick_own, pick_tx, pick_rx, mask,
    load_sem, send_sem, recv_sem, misc_tx, misc_rx, att_sem_tx, att_sem_rx, store_sem,
):
    clip = lax.axis_index("clip")
    space = lax.axis_index("space")
    core = clip % 2
    y = (clip // 2) % 2
    z = (clip // 4) % 4
    x = clip // 16
    chip = clip // 2

    def device(x, z, y, core):
        return (((x * 4 + z) * 2 + y) * 2 + core, space)

    def along(first, step):
        on_x = (1 - core) if first else core
        return device((x + step * on_x) % 4, (z + step * (1 - on_x)) % 4, y, core)

    a_up, a_down = along(True, 1), along(True, 3)
    b_up, b_down = along(False, 1), along(False, 3)
    y_pair = device(x, z, 1 - y, core)
    sibling = (clip + 1 - 2 * core, space)
    other_space = (clip, 1 - space)
    edge_chip = (chip + 2 * core + 31) % 32
    edge_to = [(edge_chip * 2, space), (edge_chip * 2 + 1, space)]
    edge_from = [(((chip + 31) % 32) * 2 + 1, space), (((chip + 1) % 32) * 2, space)]

    barrier = pltpu.get_barrier_semaphore()
    greet = [a_up, a_down, b_up, b_down, y_pair, sibling, other_space] + edge_to + edge_from
    for other in greet:
        pl.semaphore_signal(barrier, inc=1, device_id=other, device_id_type=MESH)

    loads = [
        pltpu.make_async_copy(src, dst, load_sem.at[n])
        for n, (src, dst) in enumerate(
            [
                (latent, lat),
                (group_of, g_of),
                (group_to, g_to),
                (swap16, s16),
                (edge_out, e_out),
                (wq, w.at[0]),
                (wk, w.at[1]),
                (wv, w.at[2]),
                (swap8, s8),
                (edge_in, e_in),
                (head_mask, h_mask),
                (wo, w_out),
            ]
        )
    ]
    for copy in loads:
        copy.start()

    row = lax.broadcasted_iota(jnp.int32, (48, 128), 0)
    lane = lax.broadcasted_iota(jnp.int32, (48, 128), 1)
    q_clip = (((lane >> 4) & 1) + core) & 1
    k_clip = (((row >> 4) & 1) + core) & 1
    frame = row & 15
    local = (row < 32) & (
        (k_clip == q_clip)
        | ((q_clip == 0) & (frame < EDGE))
        | ((q_clip == 1) & (frame >= FRAMES - EDGE))
    )
    left = (row >= 32) & (row < 36) & (q_clip == 0) & (chip > 0)
    right = (row >= 36) & (row < 40) & (q_clip == 1) & (chip < 31)
    mask[...] = jnp.where(local | left | right, 0.0, -jnp.inf).astype(F32)

    loads[0].wait()

    def add_rows(f, acc):
        v = lat[f].astype(F32)
        for r in range(ROWS // 8):
            acc = acc + v[8 * r : 8 * r + 8]
        return acc

    total = lax.fori_loop(0, FRAMES, add_rows, jnp.zeros((8, C), F32))
    loads[1].wait()
    loads[2].wait()
    count = FRAMES * ROWS * (C // GROUPS)
    mean_here = jnp.sum(exact_dot(total, g_of[...]), axis=0, keepdims=True) * (1.0 / count)
    mean_here = jnp.broadcast_to(mean_here, (8, 128))
    wide = exact_dot(mean_here, g_to[...])

    def add_squares(f, acc):
        v = lat[f].astype(F32)
        for r in range(ROWS // 8):
            d = v[8 * r : 8 * r + 8] - wide
            acc = acc + d * d
        return acc

    squares = lax.fori_loop(0, FRAMES, add_squares, jnp.zeros((8, C), F32))
    dev_here = jnp.sum(exact_dot(squares, g_of[...]), axis=0, keepdims=True)
    dev_here = jnp.broadcast_to(dev_here, (8, 128))
    first_row = lax.broadcasted_iota(jnp.int32, (8, 128), 0) == 0
    stat_tx[...] = jnp.where(first_row, mean_here, dev_here)

    pl.semaphore_wait(barrier, len(greet))

    def misc(n, src, dst, to):
        return pltpu.make_async_remote_copy(
            src_ref=src, dst_ref=dst, send_sem=misc_tx.at[n], recv_sem=misc_rx.at[n], device_id=to, device_id_type=MESH
        )

    stats = misc(0, stat_tx, stat_rx, other_space)
    stats.start()
    stats.wait_recv()
    mean_there = stat_rx[0:1]
    dev_there = stat_rx[1:2]
    gap = mean_here[0:1] - mean_there
    mean = 0.5 * (mean_here[0:1] + mean_there)
    var = (dev_here[0:1] + dev_there + gap * gap * (0.5 * count)) * (0.5 / count)
    scale = lax.rsqrt(var + EPS)
    both = jnp.where(first_row, jnp.broadcast_to(mean, (8, 128)), jnp.broadcast_to(scale, (8, 128)))
    both = exact_dot(both, g_to[...])
    mean_c = both[0:1]
    gain_c = both[1:2] * gain[...]
    shift_c = shift[...]

    def norm(v):
        return ((v.astype(F32) - mean_c) * gain_c + shift_c).astype(BF16)

    picked = norm(lat[picks[0, 0]]).astype(F32)
    low, high = picked[:HALF], picked[HALF:]
    pick_own[...] = jnp.where(core == 0, low, high)
    pick_tx[...] = jnp.where(core == 0, high, low)
    swap_pick = misc(1, pick_tx, pick_rx, sibling)
    swap_pick.start()

    def normalize(f, _):
        normed[f] = norm(lat[f])
        return 0

    lax.fori_loop(0, FRAMES, normalize, 0)

    swap_pick.wait_recv()
    for g in range(3):
        pair = jnp.concatenate([pick_own[8 * g : 8 * g + 8], pick_rx[8 * g : 8 * g + 8]], axis=0)
        ctx[g, 0:16, :] = pair.astype(BF16)

    def hop(i, j, s):
        if j == 0:
            if i == 0:
                src, to = (0, 0, 0), y_pair
            elif i == 1:
                src, to = (0, 0, s), a_up
            elif i == 2:
                src, to = (0, 0, s), a_down
            else:
                src, to = ((1, 0, 0), a_up) if s == 0 else ((2, 0, 1), a_down)
        elif j == 1:
            src, to = (i, 0, s), b_up
        elif j == 2:
            src, to = (i, 0, s), b_down
        else:
            src, to = ((i, 1, 0), b_up) if s == 0 else ((i, 2, 1), b_down)
        n, dst = slot_of(*src), slot_of(i, j, s)
        return pltpu.make_async_remote_copy(
            src_ref=ctx.at[:, 16 * n : 16 * n + 16, :],
            dst_ref=ctx.at[:, 16 * dst : 16 * dst + 16, :],
            send_sem=send_sem.at[dst],
            recv_sem=recv_sem.at[dst],
            device_id=to,
            device_id_type=MESH,
        )

    def start(*slots):
        for slot in slots:
            hop(*slot).start()

    start((0, 0, 1), (1, 0, 0), (2, 0, 0), (0, 1, 0), (0, 2, 0))

    loads[3].wait()

    def turn(q, _):
        rows = normed[:, pl.ds(pl.multiple_of(q * 16, 16), 16), :].reshape(256, C)
        turned[pl.ds(q * 16, 16)] = dot(s16[...], rows).astype(BF16).reshape(16, 16, C)
        return 0

    lax.fori_loop(0, 3, turn, 0)
    swap_rows = misc(2, turned.at[pl.ds(HALF * (1 - core), HALF)], sib, sibling)
    swap_rows.start()
    loads[4].wait()
    edge_rows = normed[pl.ds(12 * core, EDGE)].reshape(EDGE * ROWS, C)
    edge_tx[...] = dot(e_out[...], edge_rows).astype(BF16).reshape(2, 96, C)
    edge_sends = [
        pltpu.make_async_remote_copy(
            src_ref=edge_tx.at[k],
            dst_ref=edge_rx.at[1 - core],
            send_sem=misc_tx.at[3 + k],
            recv_sem=misc_rx.at[3 + 1 - core],
            device_id=edge_to[k],
            device_id_type=MESH,
        )
        for k in range(2)
    ]
    for copy in edge_sends:
        copy.start()

    def edge_arrived(n):
        pltpu.make_async_copy(edge_rx.at[n], edge_rx.at[n], misc_rx.at[3 + n]).wait()

    def pass_on(arrived, *slots):
        def act():
            hop(*arrived).wait_recv()
            start(*slots)

        return act

    def forward(i, s):
        return pass_on((i, 1, 0), (i, 3, 0)) if s == 0 else pass_on((i, 2, 1), (i, 3, 1))

    def run(acts, t):
        for when, act in acts:
            pl.when(t == when)(act)

    def project_query(rows, at, acts=()):
        def step(n, _):
            run(acts, n)
            cols = pl.ds(pl.multiple_of(n * TILE, TILE), TILE)
            res = dot(rows(), w[0, :, cols]) * (HEAD_DIM**-0.5)
            query[:, at : at + 16, cols] = res.astype(BF16).reshape(HALF, 16, TILE)
            return 0

        lax.fori_loop(0, TILES, step, 0)

    def project_kv(rows, at, acts=()):
        def step(t, _):
            run(acts, t)
            m = t // TILES
            cols = pl.ds(pl.multiple_of((t % TILES) * TILE, TILE), TILE)
            res = dot(rows(), w[1 + m, :, cols])
            kv[m, :, at : at + 16, cols] = res.astype(BF16).reshape(HALF, 16, TILE)
            return 0

        lax.fori_loop(0, 2 * TILES, step, 0)

    def own_rows():
        return turned[pl.ds(HALF * core, HALF)].reshape(HALF * 16, C)

    def sib_rows():
        return sib[...].reshape(HALF * 16, C)

    def ctx_rows():
        return xc[...]

    def gather_ctx(j):
        def one(g, _):
            rows = dot(s8[...], ctx[g, 128 * j : 128 * j + 128, :])
            xc[pl.ds(pl.multiple_of(g * 128, 128), 128)] = rows.astype(BF16)
            return 0

        lax.fori_loop(0, 3, one, 0)

    loads[5].wait()
    project_query(
        own_rows, 0,
        [(3, pass_on((0, 0, 1), (1, 0, 1), (2, 0, 1), (0, 1, 1), (0, 2, 1)))],
    )
    loads[6].wait()
    loads[7].wait()
    project_kv(
        own_rows, 64,
        [
            (1, pass_on((1, 0, 0), (3, 0, 0), (1, 1, 0), (1, 2, 0))),
            (2, pass_on((2, 0, 0), (2, 1, 0), (2, 2, 0))),
            (6, pass_on((2, 0, 1), (3, 0, 1), (2, 1, 1), (2, 2, 1))),
            (7, pass_on((1, 0, 1), (1, 1, 1), (1, 2, 1))),
        ],
    )
    swap_rows.wait_recv()
    project_query(
        sib_rows, 16,
        [(1, pass_on((3, 0, 0), (3, 1, 0), (3, 2, 0))), (4, pass_on((3, 0, 1), (3, 1, 1), (3, 2, 1)))],
    )
    project_kv(
        sib_rows, 80,
        [(1, forward(0, 0)), (3, forward(0, 1)), (5, forward(1, 0)), (7, forward(2, 0)), (9, forward(2, 1))],
    )
    loads[8].wait()
    gather_ctx(0)
    project_kv(ctx_rows, 0, [(1, forward(1, 1)), (4, forward(3, 0)), (7, forward(3, 1))])
    for i in range(4):
        hop(i, 1, 1).wait_recv()
        hop(i, 2, 0).wait_recv()
    gather_ctx(1)
    project_kv(ctx_rows, 16)
    gather_ctx(2)
    project_kv(ctx_rows, 32)

    loads[9].wait()
    edge_arrived(0)
    edge_arrived(1)
    edge_x[...] = dot(e_in[...], edge_rx[...].reshape(192, C)).astype(BF16)

    def edge_step(t, _):
        m = t // TILES
        cols = pl.ds(pl.multiple_of((t % TILES) * TILE, TILE), TILE)
        res = dot(edge_x[...], w[1 + m, :, cols]).reshape(HALF, 8, TILE)
        res = jnp.concatenate([res, jnp.zeros((HALF, 8, TILE), F32)], axis=1)
        kv[m, :, 96:112, cols] = res.astype(BF16)
        return 0

    lax.fori_loop(0, 2 * TILES, edge_step, 0)

    for i in range(4):
        for s in range(2):
            hop(i, 3, s).wait_recv()
    gather_ctx(3)
    project_kv(ctx_rows, 48)

    loads[10].wait()
    loads[11].wait()

    def send_att(c):
        there = pl.ds(HALF * core + 8 * c, 8)
        return pltpu.make_async_remote_copy(
            src_ref=att_tx.at[8 * c : 8 * c + 8],
            dst_ref=att.at[there],
            send_sem=att_sem_tx.at[c],
            recv_sem=att_sem_rx.at[c],
            device_id=sibling,
            device_id_type=MESH,
        )

    def attend(p, _):
        half = lax.broadcasted_iota(jnp.int32, (32, 128), 1) < HEAD_DIM
        for h in range(TILES):
            cols = slice(h * TILE, (h + 1) * TILE)
            q = query[p, :, cols]
            q = jnp.concatenate([q] * 4, axis=0) * h_mask[...]
            scores = lax.dot_general(
                kv[0, p, :, cols], q, (((1,), (1,)), ((), ())), preferred_element_type=F32
            )
            scores = jnp.concatenate([scores[:64], scores[64:] + mask[...]], axis=0)
            top = jnp.max(scores, axis=0, keepdims=True)
            expo = jnp.exp(scores - top)
            share = 1.0 / jnp.sum(expo, axis=0, keepdims=True)
            weights = (expo * share).astype(BF16)
            mixed = lax.dot_general(
                weights, kv[1, p, :, cols], (((0,), (0,)), ((), ())), preferred_element_type=F32
            )
            for t in range(2):
                lanes = slice(128 * t, 128 * t + 128)
                lo = mixed[64 * t : 64 * t + 32, lanes]
                hi = mixed[64 * t + 32 : 64 * t + 64, lanes]
                both = jnp.where(half, lo, hi).astype(BF16)
                to = slice(h * TILE + 128 * t, h * TILE + 128 * t + 128)
                att[HALF * core + p, :, to] = both[:16]
                att_tx[p, :, to] = both[16:]
        return 0

    for c in range(3):
        lax.fori_loop(8 * c, 8 * c + 8, attend, 0)
        send_att(c).start()
    for c in range(3):
        there = pl.ds(HALF * (1 - core) + 8 * c, 8)
        pltpu.make_async_copy(att.at[there], att.at[there], att_sem_rx.at[c]).wait()

    def turn_back(q, _):
        rows = att[pl.ds(q * 16, 16)].reshape(256, C)
        turned_rows = dot(s16[...], rows).astype(BF16)
        normed[:, pl.ds(pl.multiple_of(q * 16, 16), 16), :] = turned_rows.reshape(16, 16, C)
        return 0

    lax.fori_loop(0, 3, turn_back, 0)

    def project_out(n, _):
        cols = pl.ds(pl.multiple_of(n * TILE, TILE), TILE)
        res = dot(normed[...].reshape(FRAMES * ROWS, C), w_out[:, cols])
        res = lat[:, :, cols].astype(F32) + res.reshape(FRAMES, ROWS, TILE) + out_bias[:, cols].reshape(1, 1, TILE)
        result[:, :, cols] = res.astype(BF16)
        return 0

    lax.fori_loop(0, TILES, project_out, 0)
    store = pltpu.make_async_copy(result, out, store_sem)
    store.start()

    stats.wait_send()
    swap_pick.wait_send()
    swap_rows.wait_send()
    for copy in edge_sends:
        copy.wait_send()
    for j in range(4):
        for i in range(4):
            for s in range(2):
                if (i, j, s) != (0, 0, 0):
                    hop(i, j, s).wait_send()
    for c in range(3):
        send_att(c).wait_send()
    store.wait()


def local(latent, gn_gain, gn_bias, w_query, w_key, w_value, w_out, out_bias, context_frames):
    consts = [
        jnp.asarray(SWAP16, BF16),
        jnp.asarray(SWAP8, BF16),
        jnp.asarray(EDGE_OUT, BF16),
        jnp.asarray(EDGE_IN, BF16),
        jnp.asarray(GROUP_OF, F32),
        jnp.asarray(GROUP_OF.T.copy(), F32),
        jnp.asarray(HEAD_MASK, BF16),
    ]
    any_ = pl.BlockSpec(memory_space=pl.ANY)
    vmem = pl.BlockSpec(memory_space=pltpu.VMEM)
    smem = pl.BlockSpec(memory_space=pltpu.SMEM)
    dma = pltpu.SemaphoreType.DMA
    return pl.pallas_call(
        kernel,
        out_shape=jax.ShapeDtypeStruct((FRAMES, ROWS, C), BF16),
        in_specs=[any_, vmem, vmem, any_, any_, any_, any_, vmem, smem] + [any_] * 7,
        out_specs=any_,
        scratch_shapes=[
            pltpu.VMEM((FRAMES, ROWS, C), BF16),
            pltpu.VMEM((FRAMES, ROWS, C), BF16),
            pltpu.VMEM((ROWS, FRAMES, C), BF16),
            pltpu.VMEM((HALF, FRAMES, C), BF16),
            pltpu.VMEM((3, 512, C), BF16),
            pltpu.VMEM((HALF * 16, C), BF16),
            pltpu.VMEM((2, 96, C), BF16),
            pltpu.VMEM((2, 96, C), BF16),
            pltpu.VMEM((192, C), BF16),
            pltpu.VMEM((HALF, 32, C), BF16),
            pltpu.VMEM((2, HALF, KEYS, C), BF16),
            pltpu.VMEM((ROWS, FRAMES, C), BF16),
            pltpu.VMEM((HALF, FRAMES, C), BF16),
            pltpu.VMEM((FRAMES, ROWS, C), BF16),
            pltpu.VMEM((3, C, C), BF16),
            pltpu.VMEM((C, C), BF16),
            pltpu.VMEM((256, 256), BF16),
            pltpu.VMEM((128, 128), BF16),
            pltpu.VMEM((192, 192), BF16),
            pltpu.VMEM((192, 192), BF16),
            pltpu.VMEM((C, 128), F32),
            pltpu.VMEM((128, C), F32),
            pltpu.VMEM((128, TILE), BF16),
            pltpu.VMEM((8, 128), F32),
            pltpu.VMEM((8, 128), F32),
            pltpu.VMEM((HALF, C), F32),
            pltpu.VMEM((HALF, C), F32),
            pltpu.VMEM((HALF, C), F32),
            pltpu.VMEM((48, 128), F32),
            dma((12,)),
            dma((32,)),
            dma((32,)),
            dma((5,)),
            dma((5,)),
            dma((3,)),
            dma((3,)),
            dma,
        ],
        compiler_params=pltpu.CompilerParams(
            collective_id=0, has_side_effects=True, vmem_limit_bytes=60 * 1024 * 1024
        ),
        cost_estimate=pl.CostEstimate(flops=25 * 10**9, bytes_accessed=18 * 10**6, transcendentals=2 * 10**6),
    )(
        latent, gn_gain.reshape(1, C), gn_bias.reshape(1, C), w_query, w_key, w_value, w_out,
        out_bias.reshape(1, C), context_frames, *consts,
    )


def solution(mesh):
    placed = (P("clip", "space", None), P(), P(), P(), P(), P(), P(), P(), P("clip", None))
    return jax.shard_map(
        local, mesh=mesh, in_specs=placed, out_specs=P("clip", "space", None), check_vma=False
    )
```

time: 281 us -> 101 us (0.36)
  waiting for transfers between devices: 116 us -> 0 us
  Pallas kernels: 0 us -> 92.4 us
  local copies, waits for them, and re-layouts: 64.2 us -> 6.81 us
  matrix products: 39.9 us -> 0 us
  other arithmetic: 25.3 us -> 0 us
  between operations: 14.4 us -> 0.66 us
  blocking collectives: 11.4 us -> 0 us
  starting transfers between devices: 8.22 us -> 0 us
    all_gather x1 -> x0, waiting for transfers between devices: 106 us -> none  [local(): lax.all_gather(jnp.take(stacked, picks, axis=1), 'clip', axis=1, tiled=True)]
    pallas_call x0 -> x1, Pallas kernels: none -> 92.4 us  [local(): pl.pallas_call(kernel, out_shape=jax.ShapeDtypeStruct((FRAMES, ROWS, C),...]
    slice x3 -> x0, local copies, waits for them, and re-layouts: 45 us -> none  [the longest x2 26.4 us: local(): k_heads = gathered[0].reshape(count_keys, rows, heads, HEAD_DIM)]
    dot_general x6 -> x0, matrix products: 39.9 us -> none  [the longest x1 14.3 us: local(): jnp.einsum('phfk,kphd->fphd', weights, v_heads, preferred_element_type=jn...]
    convert_element_type x2 -> x0, local copies, waits for them, and re-layouts: 11.9 us -> none  [local(): attended = attended.reshape(frames * rows, width).astype(jnp.bfloat16)]
    psum x2 -> x0, blocking collectives: 11.4 us -> none  [the longest x1 6.05 us: local(): mean = lax.psum(jnp.sum(x, axis=(0, 1, 3)), 'space') / count]
    ppermute x2 -> x0, waiting for transfers between devices: 10.9 us -> none  [the longest x1 10.2 us: with_halo(): lax.ppermute(head, axis, [((i + 1) % count, i) for i in range(ends)])]
    concatenate x2 -> x0, other arithmetic: 9.66 us -> none  [the longest x1 9.58 us: local(): gathered = jnp.concatenate([padded, remote], axis=1)]
  transfers between devices with their start and end apart: 3 -> 0, of which waited for: 3 -> 0; matrix products, arithmetic and copies ran while one was open for 5% -> 0% of each run, Pallas kernels for 0% -> 0%
where the time goes in v1:
time: 101 us; the launch traced here: 99.8 us
  Pallas kernels  92.4 us (91%)
  local copies, waits for them, and re-layouts  6.81 us (7%)
    pallas_call x1, Pallas kernels, local(): pl.pallas_call(kernel, out_shape=jax.ShapeDtypeStruct((FRAMES, ROWS, C),...  92.4 us
    unnamed x1, local copies, waits for them, and re-layouts  2.94 us

profile of v1, /device:TPU:1, one launch (start us, length us, event | category | flops | bytes accessed | tf_op | source)
XLA Modules:
  0.0 99.8 jit_solution(14853896501107206024)
XLA Ops:
  0.7 1.3 %reshape.9.gain = f32[1,1280]{1,0:T(1,128)} reshape(f32[1280]{0:T(1024)} %param.17) | data formatting | bytes 10240 | tf_op jit(solution)/shard_map/reshape | solution.py:526
  1.9 1.3 %reshape.10.shift = f32[1,1280]{1,0:T(1,128)} reshape(f32[1280]{0:T(1024)} %param.18) | data formatting | bytes 10240 | tf_op jit(solution)/shard_map/reshape | solution.py:526
  3.2 1.3 %reshape.11.out_bias = f32[1,1280]{1,0:T(1,128)} reshape(f32[1280]{0:T(1024)} %param.23) | data formatting | bytes 10240 | tf_op jit(solution)/shard_map/reshape | solution.py:527
  4.5 92.4 %shard_map.154 = bf16[16,48,1280]{2,1,0:T(8,128)(2,1)} custom-call(bf16[16,48,1280]{2,1,0:T(8,128)(2,1)} %latent.1, f32[1,1280]{1,0:T(1,128)} %reshape.9.gain, f32[1,1280]{1,0:T(1,128)} %reshape.10.shift, bf16[1280,1280]{1,0:T(8,128)(2,1)} %wq.1, bf16[1280,1280]{1,0:T(8,128)(2,1)} %wk.1, bf16[1280,1280]{1,0:T(8,128)(2,1)} %wv.1, bf16[1280,1280]{1,0:T(8,128)(2,1)} %wo.1, ...), custom_call_target="tpu_custom_call" | custom-call | flops 24999999488 | bytes 18000000 | tf_op jit(solution)/shard_map/pallas_call | solution.py:477
  96.9 2.9 %copy.19 = bf16[16,48,1280]{2,1,0:T(8,128)(2,1)} copy(bf16[16,48,1280]{2,1,0:T(8,128)(2,1)} %shard_map.154) | data formatting | bytes 3932160

commit v2 on v1

--- a/solution.py
+++ b/solution.py
@@ -183,8 +183,8 @@
     both = jnp.where(first_row, jnp.broadcast_to(mean, (8, 128)), jnp.broadcast_to(scale, (8, 128)))
     both = exact_dot(both, g_to[...])
     mean_c = both[0:1]
-    gain_c = both[1:2] * gain[...]
-    shift_c = shift[...]
+    gain_c = both[1:2] * gain[...].reshape(1, C)
+    shift_c = shift[...].reshape(1, C)
 
     def norm(v):
         return ((v.astype(F32) - mean_c) * gain_c + shift_c).astype(BF16)
@@ -241,12 +241,9 @@
 
     loads[3].wait()
 
-    def turn(q, _):
-        rows = normed[:, pl.ds(pl.multiple_of(q * 16, 16), 16), :].reshape(256, C)
-        turned[pl.ds(q * 16, 16)] = dot(s16[...], rows).astype(BF16).reshape(16, 16, C)
-        return 0
-
-    lax.fori_loop(0, 3, turn, 0)
+    for q in range(3):
+        rows = normed[:, 16 * q : 16 * q + 16, :].reshape(256, C)
+        turned[16 * q : 16 * q + 16] = dot(s16[...], rows).astype(BF16).reshape(16, 16, C)
     swap_rows = misc(2, turned.at[pl.ds(HALF * (1 - core), HALF)], sib, sibling)
     swap_rows.start()
     loads[4].wait()
@@ -279,30 +276,23 @@
     def forward(i, s):
         return pass_on((i, 1, 0), (i, 3, 0)) if s == 0 else pass_on((i, 2, 1), (i, 3, 1))
 
-    def run(acts, t):
-        for when, act in acts:
-            pl.when(t == when)(act)
-
-    def project_query(rows, at, acts=()):
-        def step(n, _):
-            run(acts, n)
-            cols = pl.ds(pl.multiple_of(n * TILE, TILE), TILE)
-            res = dot(rows(), w[0, :, cols]) * (HEAD_DIM**-0.5)
-            query[:, at : at + 16, cols] = res.astype(BF16).reshape(HALF, 16, TILE)
+    def project(rows, m, dst, at, factor=None):
+        res = dot(rows, w[m])
+        if factor is not None:
+            res = res * factor
+        dst[:, at : at + 16, :] = res.astype(BF16).reshape(HALF, 16, C)
+
+    def project_query(rows, at):
+        project(rows, 0, query, at, HEAD_DIM**-0.5)
+
+    def project_kv(rows, at, acts=()):
+        def step(m, _):
+            for n, act in enumerate(acts):
+                pl.when(m == n)(act)
+            project(rows(), 1 + m, kv.at[m], at)
             return 0
 
-        lax.fori_loop(0, TILES, step, 0)
-
-    def project_kv(rows, at, acts=()):
-        def step(t, _):
-            run(acts, t)
-            m = t // TILES
-            cols = pl.ds(pl.multiple_of((t % TILES) * TILE, TILE), TILE)
-            res = dot(rows(), w[1 + m, :, cols])
-            kv[m, :, at : at + 16, cols] = res.astype(BF16).reshape(HALF, 16, TILE)
-            return 0
-
-        lax.fori_loop(0, 2 * TILES, step, 0)
+        lax.fori_loop(0, 2, step, 0)
 
     def own_rows():
         return turned[pl.ds(HALF * core, HALF)].reshape(HALF * 16, C)
@@ -314,64 +304,75 @@
         return xc[...]
 
     def gather_ctx(j):
-        def one(g, _):
+        for g in range(3):
             rows = dot(s8[...], ctx[g, 128 * j : 128 * j + 128, :])
-            xc[pl.ds(pl.multiple_of(g * 128, 128), 128)] = rows.astype(BF16)
-            return 0
-
-        lax.fori_loop(0, 3, one, 0)
+            xc[128 * g : 128 * g + 128] = rows.astype(BF16)
+
+    def many(*acts):
+        def act():
+            for one in acts:
+                one()
+
+        return act
 
     loads[5].wait()
-    project_query(
-        own_rows, 0,
-        [(3, pass_on((0, 0, 1), (1, 0, 1), (2, 0, 1), (0, 1, 1), (0, 2, 1)))],
-    )
+    project_query(own_rows(), 0)
     loads[6].wait()
     loads[7].wait()
     project_kv(
         own_rows, 64,
         [
-            (1, pass_on((1, 0, 0), (3, 0, 0), (1, 1, 0), (1, 2, 0))),
-            (2, pass_on((2, 0, 0), (2, 1, 0), (2, 2, 0))),
-            (6, pass_on((2, 0, 1), (3, 0, 1), (2, 1, 1), (2, 2, 1))),
-            (7, pass_on((1, 0, 1), (1, 1, 1), (1, 2, 1))),
+            pass_on((0, 0, 1), (1, 0, 1), (2, 0, 1), (0, 1, 1), (0, 2, 1)),
+            many(
+                pass_on((1, 0, 0), (3, 0, 0), (1, 1, 0), (1, 2, 0)),
+                pass_on((2, 0, 0), (2, 1, 0), (2, 2, 0)),
+            ),
         ],
     )
     swap_rows.wait_recv()
-    project_query(
-        sib_rows, 16,
-        [(1, pass_on((3, 0, 0), (3, 1, 0), (3, 2, 0))), (4, pass_on((3, 0, 1), (3, 1, 1), (3, 2, 1)))],
-    )
+    project_query(sib_rows(), 16)
     project_kv(
         sib_rows, 80,
-        [(1, forward(0, 0)), (3, forward(0, 1)), (5, forward(1, 0)), (7, forward(2, 0)), (9, forward(2, 1))],
+        [
+            many(
+                pass_on((2, 0, 1), (3, 0, 1), (2, 1, 1), (2, 2, 1)),
+                pass_on((1, 0, 1), (1, 1, 1), (1, 2, 1)),
+            ),
+            many(
+                pass_on((3, 0, 0), (3, 1, 0), (3, 2, 0)),
+                forward(0, 0),
+            ),
+        ],
     )
+    pass_on((3, 0, 1), (3, 1, 1), (3, 2, 1))()
+    forward(0, 1)()
     loads[8].wait()
     gather_ctx(0)
-    project_kv(ctx_rows, 0, [(1, forward(1, 1)), (4, forward(3, 0)), (7, forward(3, 1))])
-    for i in range(4):
-        hop(i, 1, 1).wait_recv()
-        hop(i, 2, 0).wait_recv()
-    gather_ctx(1)
-    project_kv(ctx_rows, 16)
-    gather_ctx(2)
-    project_kv(ctx_rows, 32)
+    project_kv(ctx_rows, 0, [forward(1, 0), many(forward(2, 0), forward(2, 1))])
 
     loads[9].wait()
     edge_arrived(0)
     edge_arrived(1)
     edge_x[...] = dot(e_in[...], edge_rx[...].reshape(192, C)).astype(BF16)
 
-    def edge_step(t, _):
-        m = t // TILES
-        cols = pl.ds(pl.multiple_of((t % TILES) * TILE, TILE), TILE)
-        res = dot(edge_x[...], w[1 + m, :, cols]).reshape(HALF, 8, TILE)
-        res = jnp.concatenate([res, jnp.zeros((HALF, 8, TILE), F32)], axis=1)
-        kv[m, :, 96:112, cols] = res.astype(BF16)
+    def edge_step(m, _):
+        pl.when(m == 0)(forward(1, 1))
+        pl.when(m == 1)(many(forward(3, 0), forward(3, 1)))
+        res = dot(edge_x[...], w[1 + m]).reshape(HALF, 8, C)
+        res = jnp.concatenate([res, jnp.zeros((HALF, 8, C), F32)], axis=1)
+        kv[m, :, 96:112, :] = res.astype(BF16)
         return 0
 
-    lax.fori_loop(0, 2 * TILES, edge_step, 0)
-
+    lax.fori_loop(0, 2, edge_step, 0)
+
+    for i in range(4):
+        hop(i, 1, 1).wait_recv()
+    gather_ctx(1)
+    project_kv(ctx_rows, 16)
+    for i in range(4):
+        hop(i, 2, 0).wait_recv()
+    gather_ctx(2)
+    project_kv(ctx_rows, 32)
     for i in range(4):
         for s in range(2):
             hop(i, 3, s).wait_recv()
@@ -392,56 +393,48 @@
             device_id_type=MESH,
         )
 
-    def attend(p, _):
+    def attend(block, _):
         half = lax.broadcasted_iota(jnp.int32, (32, 128), 1) < HEAD_DIM
-        for h in range(TILES):
-            cols = slice(h * TILE, (h + 1) * TILE)
-            q = query[p, :, cols]
-            q = jnp.concatenate([q] * 4, axis=0) * h_mask[...]
-            scores = lax.dot_general(
-                kv[0, p, :, cols], q, (((1,), (1,)), ((), ())), preferred_element_type=F32
+        units = [(block * 4 + n, h) for n in range(4) for h in range(TILES)]
+        cols = [slice(h * TILE, (h + 1) * TILE) for h in range(TILES)]
+        scores, weights, mixed = [], [], []
+        for p, h in units:
+            q = jnp.concatenate([query[p, :, cols[h]]] * 4, axis=0) * h_mask[...]
+            scores.append(
+                lax.dot_general(kv[0, p, :, cols[h]], q, (((1,), (1,)), ((), ())), preferred_element_type=F32)
             )
-            scores = jnp.concatenate([scores[:64], scores[64:] + mask[...]], axis=0)
-            top = jnp.max(scores, axis=0, keepdims=True)
-            expo = jnp.exp(scores - top)
+        for s in scores:
+            s = jnp.concatenate([s[:64], s[64:] + mask[...]], axis=0)
+            expo = jnp.exp(s - jnp.max(s, axis=0, keepdims=True))
             share = 1.0 / jnp.sum(expo, axis=0, keepdims=True)
-            weights = (expo * share).astype(BF16)
-            mixed = lax.dot_general(
-                weights, kv[1, p, :, cols], (((0,), (0,)), ((), ())), preferred_element_type=F32
+            weights.append((expo * share).astype(BF16))
+        for (p, h), s in zip(units, weights):
+            mixed.append(
+                lax.dot_general(s, kv[1, p, :, cols[h]], (((0,), (0,)), ((), ())), preferred_element_type=F32)
             )
+        for (p, h), m in zip(units, mixed):
             for t in range(2):
                 lanes = slice(128 * t, 128 * t + 128)
-                lo = mixed[64 * t : 64 * t + 32, lanes]
-                hi = mixed[64 * t + 32 : 64 * t + 64, lanes]
-                both = jnp.where(half, lo, hi).astype(BF16)
+                both = jnp.where(half, m[64 * t : 64 * t + 32, lanes], m[64 * t + 32 : 64 * t + 64, lanes])
+                both = both.astype(BF16)
                 to = slice(h * TILE + 128 * t, h * TILE + 128 * t + 128)
                 att[HALF * core + p, :, to] = both[:16]
                 att_tx[p, :, to] = both[16:]
         return 0
 
     for c in range(3):
-        lax.fori_loop(8 * c, 8 * c + 8, attend, 0)
+        lax.fori_loop(2 * c, 2 * c + 2, attend, 0)
         send_att(c).start()
     for c in range(3):
         there = pl.ds(HALF * (1 - core) + 8 * c, 8)
         pltpu.make_async_copy(att.at[there], att.at[there], att_sem_rx.at[c]).wait()
 
-    def turn_back(q, _):
-        rows = att[pl.ds(q * 16, 16)].reshape(256, C)
-        turned_rows = dot(s16[...], rows).astype(BF16)
-        normed[:, pl.ds(pl.multiple_of(q * 16, 16), 16), :] = turned_rows.reshape(16, 16, C)
-        return 0
-
-    lax.fori_loop(0, 3, turn_back, 0)
-
-    def project_out(n, _):
-        cols = pl.ds(pl.multiple_of(n * TILE, TILE), TILE)
-        res = dot(normed[...].reshape(FRAMES * ROWS, C), w_out[:, cols])
-        res = lat[:, :, cols].astype(F32) + res.reshape(FRAMES, ROWS, TILE) + out_bias[:, cols].reshape(1, 1, TILE)
-        result[:, :, cols] = res.astype(BF16)
-        return 0
-
-    lax.fori_loop(0, TILES, project_out, 0)
+    for q in range(3):
+        rows = dot(s16[...], att[16 * q : 16 * q + 16].reshape(256, C))
+        normed[:, 16 * q : 16 * q + 16, :] = rows.astype(BF16).reshape(16, 16, C)
+    res = dot(normed[...].reshape(FRAMES * ROWS, C), w_out[...])
+    res = lat[...].astype(F32) + res.reshape(FRAMES, ROWS, C) + out_bias[...].reshape(1, 1, C)
+    result[...] = res.astype(BF16)
     store = pltpu.make_async_copy(result, out, store_sem)
     store.start()
 
@@ -523,8 +516,8 @@
         ),
         cost_estimate=pl.CostEstimate(flops=25 * 10**9, bytes_accessed=18 * 10**6, transcendentals=2 * 10**6),
     )(
-        latent, gn_gain.reshape(1, C), gn_bias.reshape(1, C), w_query, w_key, w_value, w_out,
-        out_bias.reshape(1, C), context_frames, *consts,
+        latent, gn_gain, gn_bias, w_query, w_key, w_value, w_out,
+        out_bias, context_frames, *consts,
     )
 
 

time: 101 us -> 68.5 us (0.68)
  the two profiles are of different devices: /device:TPU:1 before, /device:TPU:5 now
where the time goes in v2:
time: 68.5 us; the launch traced here: 68.3 us
  Pallas kernels  64.7 us (94%)
  local copies, waits for them, and re-layouts  2.94 us (4%)
    pallas_call x1, Pallas kernels, local(): pl.pallas_call(kernel, out_shape=jax.ShapeDtypeStruct((FRAMES, ROWS, C),...  64.7 us
    unnamed x1, local copies, waits for them, and re-layouts  2.94 us

profile of v2, /device:TPU:5, one launch (start us, length us, event | category | flops | bytes accessed | tf_op | source)
XLA Modules:
  0.0 68.3 jit_solution(1146037696286406347)
XLA Ops:
  0.7 64.7 %shard_map.154 = bf16[16,48,1280]{2,1,0:T(8,128)(2,1)} custom-call(bf16[16,48,1280]{2,1,0:T(8,128)(2,1)} %latent.1, f32[1280]{0:T(1024)} %gain.1, f32[1280]{0:T(1024)} %shift.1, bf16[1280,1280]{1,0:T(8,128)(2,1)} %wq.1, bf16[1280,1280]{1,0:T(8,128)(2,1)} %wk.1, bf16[1280,1280]{1,0:T(8,128)(2,1)} %wv.1, bf16[1280,1280]{1,0:T(8,128)(2,1)} %wo.1, ...), custom_call_target="tpu_custom_call" | custom-call | flops 24999999488 | bytes 18000000 | tf_op jit(solution)/shard_map/pallas_call | solution.py:470
  65.4 2.9 %copy.19 = bf16[16,48,1280]{2,1,0:T(8,128)(2,1)} copy(bf16[16,48,1280]{2,1,0:T(8,128)(2,1)} %shard_map.154) | data formatting | bytes 3932160

commit v3 on v2

v3 whole, which is shorter than its diff:
```python
import numpy as np

import jax
import jax.numpy as jnp
from jax import lax
from jax.experimental import pallas as pl
from jax.experimental.pallas import tpu as pltpu
from jax.sharding import PartitionSpec as P

C = 1280
HEAD_DIM = 64
GROUPS = 32
FRAMES = 16
EDGE = 4
EPS = 1e-06
ROWS = 48
HALF = 24
KEYS = 112
TILE = 256
TILES = C // TILE
MESH = pl.DeviceIdType.MESH
F32, BF16 = jnp.float32, jnp.bfloat16


def swap_matrix(outer, inner, blocks=1):
    n = outer * inner
    m = np.zeros((n, n), np.float32)
    for i in range(outer):
        for j in range(inner):
            m[j * outer + i, i * inner + j] = 1
    return m


def edge_merge():
    m = np.zeros((192, 192), np.float32)
    for side in range(2):
        for p in range(HALF):
            for f in range(EDGE):
                m[p * 8 + side * 4 + f, side * 96 + p * 4 + f] = 1
    return m


SWAP16 = swap_matrix(16, 16)
SWAP8 = swap_matrix(16, 8)
EDGE_OUT = swap_matrix(EDGE, ROWS)
EDGE_IN = edge_merge()
GROUP_OF = np.zeros((C, 128), np.float32)
GROUP_OF[np.arange(C), np.arange(C) // (C // GROUPS)] = 1
HEAD_MASK = np.zeros((128, TILE), np.float32)
for _h in range(4):
    HEAD_MASK[_h * 32 : _h * 32 + 32, _h * 64 : _h * 64 + 64] = 1


def dot(a, b):
    return jnp.dot(a, b, preferred_element_type=F32)


def exact_dot(a, b):
    high = a.astype(BF16).astype(F32)
    mid = (a - high).astype(BF16).astype(F32)
    low = a - high - mid
    n = a.shape[0]
    res = dot(jnp.concatenate([high, mid, low], axis=0).astype(BF16), b)
    return res[:n] + res[n : 2 * n] + res[2 * n :]


def slot_of(i, j, s):
    return j * 8 + i * 2 + s


def kernel(
    latent, gain_in, shift_in, wq, wk, wv, wo, bias_in, picks, swap16, swap8, edge_out, edge_in, group_of, group_to, head_mask,
    out,
    lat, turned, sib, own_x, ctx, xc, edge_tx, edge_relay, edge_rx, edge_x, query, kv, att, att_tx, result, w, w_out,
    s16, s8, e_out, e_in, g_of, g_to, h_mask, gain, shift, out_bias, stat_tx, stat_rx, final_tx, final_rx, pick_own, pick_tx, pick_rx, mask,
    load_sem, send_sem, recv_sem, misc_tx, misc_rx, stat_sem_tx, stat_sem_rx, final_sem_tx, final_sem_rx, relay_rx, att_sem_tx, att_sem_rx, store_sem,
):
    clip = lax.axis_index("clip")
    space = lax.axis_index("space")
    core = clip % 2
    y = (clip // 2) % 2
    z = (clip // 4) % 4
    x = clip // 16
    chip = clip // 2

    def device(x, z, y, core):
        return (((x * 4 + z) * 2 + y) * 2 + core, space)

    def along(first, step):
        on_x = (1 - core) if first else core
        return device((x + step * on_x) % 4, (z + step * (1 - on_x)) % 4, y, core)

    a_up, a_down = along(True, 1), along(True, 3)
    b_up, b_down = along(False, 1), along(False, 3)
    y_pair = device(x, z, 1 - y, core)
    sibling = (clip + 1 - 2 * core, space)
    stats_to = [(clip, 1 - space), sibling, (clip + 1 - 2 * core, 1 - space)]
    edge_chip = (chip + 2 * core + 31) % 32
    edge_to = [(edge_chip * 2, space), (edge_chip * 2 + 1, space)]
    edge_from = [(((chip + 31) % 32) * 2 + 1, space), (((chip + 1) % 32) * 2, space)]

    relay_z = (z + 2 * y + 3) % 4
    relay_to = [device(x, relay_z, y, k) for k in range(2)]
    origin_z = (z + 5 - 2 * y) % 4
    relay_from = [device(x, origin_z, y, k) for k in range(2)]
    pass_chip = ((x * 4 + origin_z) * 2 + y + 2 * y + 31) % 32
    pass_to = (pass_chip * 2 + core, space)
    near = (chip + 2 * y + 31) % 32
    pass_from = device(near // 8, ((near // 2) % 4 + 2 * (1 - y) + 3) % 4, 1 - y, core)

    edge_up = core * y * (1 - (z + 2) // 3)
    edge_down = core * (1 - y) * (z // 3)

    barrier = pltpu.get_barrier_semaphore()
    greet = [a_up, a_down, b_up, b_down, y_pair] + stats_to + edge_to + edge_from
    greet += relay_to + relay_from + [pass_to, pass_from]
    for other in greet:
        pl.semaphore_signal(barrier, inc=1, device_id=other, device_id_type=MESH)

    loads = [
        pltpu.make_async_copy(src, dst, load_sem.at[n])
        for n, (src, dst) in enumerate(
            [
                (latent, lat),
                (group_of, g_of),
                (group_to, g_to),
                (swap16, s16),
                (edge_out, e_out),
                (gain_in, gain),
                (shift_in, shift),
                (bias_in, out_bias),
                (wq, w.at[0]),
                (wk, w.at[1]),
                (wv, w.at[2]),
                (swap8, s8),
                (edge_in, e_in),
                (head_mask, h_mask),
                (wo, w_out),
            ]
        )
    ]
    for copy in loads[:8]:
        copy.start()

    row = lax.broadcasted_iota(jnp.int32, (48, 128), 0)
    lane = lax.broadcasted_iota(jnp.int32, (48, 128), 1)
    q_clip = (((lane >> 4) & 1) + core) & 1
    k_clip = (((row >> 4) & 1) + core) & 1
    frame = row & 15
    local = (row < 32) & (
        (k_clip == q_clip)
        | ((q_clip == 0) & (frame < EDGE))
        | ((q_clip == 1) & (frame >= FRAMES - EDGE))
    )
    left = (row >= 32) & (row < 36) & (q_clip == 0) & (chip > 0)
    right = (row >= 36) & (row < 40) & (q_clip == 1) & (chip < 31)
    mask[...] = jnp.where(local | left | right, 0.0, -jnp.inf).astype(F32)

    loads[0].wait()
    for copy in loads[8:]:
        copy.start()

    def add_rows(f, acc):
        v = lat[f].astype(F32)
        for r in range(ROWS // 8):
            acc = acc + v[8 * r : 8 * r + 8]
        return acc

    total = lax.fori_loop(0, FRAMES, add_rows, jnp.zeros((8, C), F32))
    loads[1].wait()
    loads[2].wait()
    count = FRAMES * ROWS * (C // GROUPS)
    mean_here = jnp.sum(exact_dot(total, g_of[...]), axis=0, keepdims=True) * (1.0 / count)
    mean_here = jnp.broadcast_to(mean_here, (8, 128))
    wide = exact_dot(mean_here, g_to[...])

    def add_squares(f, acc):
        v = lat[f].astype(F32)
        for r in range(ROWS // 8):
            d = v[8 * r : 8 * r + 8] - wide
            acc = acc + d * d
        return acc

    squares = lax.fori_loop(0, FRAMES, add_squares, jnp.zeros((8, C), F32))
    dev_here = jnp.sum(exact_dot(squares, g_of[...]), axis=0, keepdims=True)
    dev_here = jnp.broadcast_to(dev_here, (8, 128))
    first_row = lax.broadcasted_iota(jnp.int32, (8, 128), 0) == 0
    stat_tx[...] = jnp.where(first_row, mean_here, dev_here)

    picked = lat[picks[0, 0]].astype(F32)
    low, high = picked[:HALF], picked[HALF:]
    pick_own[...] = jnp.where(core == 0, low, high)
    pick_tx[...] = jnp.where(core == 0, high, low)

    pl.semaphore_wait(barrier, len(greet))

    def misc(n, src, dst, to):
        return pltpu.make_async_remote_copy(
            src_ref=src, dst_ref=dst, send_sem=misc_tx.at[n], recv_sem=misc_rx.at[n], device_id=to, device_id_type=MESH
        )

    stats = [
        pltpu.make_async_remote_copy(
            src_ref=stat_tx,
            dst_ref=stat_rx.at[n],
            send_sem=stat_sem_tx.at[n],
            recv_sem=stat_sem_rx.at[n],
            device_id=to,
            device_id_type=MESH,
        )
        for n, to in enumerate(stats_to)
    ]
    for copy in stats:
        copy.start()
    swap_pick = misc(1, pick_tx, pick_rx, sibling)
    swap_pick.start()

    loads[4].wait()
    edge_rows = lat[pl.ds(12 * core, EDGE)].reshape(EDGE * ROWS, C)
    edge_tx[...] = dot(e_out[...], edge_rows).astype(BF16).reshape(2, 96, C)
    relays = [
        pltpu.make_async_remote_copy(
            src_ref=edge_tx.at[k],
            dst_ref=edge_relay,
            send_sem=misc_tx.at[3 + k],
            recv_sem=relay_rx,
            device_id=relay_to[k],
            device_id_type=MESH,
        )
        for k in range(2)
    ]
    directs = [
        pltpu.make_async_remote_copy(
            src_ref=edge_tx.at[k],
            dst_ref=edge_rx.at[1 - core],
            send_sem=misc_tx.at[5 + k],
            recv_sem=misc_rx.at[3 + 1 - core],
            device_id=edge_to[k],
            device_id_type=MESH,
        )
        for k in range(2)
    ]
    passing = pltpu.make_async_remote_copy(
        src_ref=edge_relay,
        dst_ref=edge_rx.at[1 - y],
        send_sem=misc_tx.at[7],
        recv_sem=misc_rx.at[3 + 1 - y],
        device_id=pass_to,
        device_id_type=MESH,
    )

    @pl.when(core == y)
    def _():
        for copy in relays:
            copy.start()

    def send_edges():
        @pl.when(core != y)
        def _():
            for copy in directs:
                copy.start()

        relays[0].wait_recv()
        passing.start()

    loads[3].wait()
    for q in range(3):
        rows = lat[:, 16 * q : 16 * q + 16, :].reshape(256, C)
        turned[16 * q : 16 * q + 16] = dot(s16[...], rows).astype(BF16).reshape(16, 16, C)
    swap_rows = misc(2, turned.at[pl.ds(HALF * (1 - core), HALF)], sib, sibling)
    swap_rows.start()

    for copy in stats:
        copy.wait_recv()

    loads[5].wait()
    loads[6].wait()

    def combine(one, two):
        mean_one, mean_two = one[0:1], two[0:1]
        gap = mean_one - mean_two
        var = (one[1:2] + two[1:2] + gap * gap * (0.5 * count)) * (0.5 / count)
        return [0.5 * (mean_one + mean_two), lax.rsqrt(var + EPS)]

    table = combine(stat_tx[...], stat_rx[0]) + combine(stat_rx[1], stat_rx[2])
    final_tx[...] = jnp.concatenate(table + table, axis=0)
    final_sends = [
        pltpu.make_async_remote_copy(
            src_ref=final_tx,
            dst_ref=final_rx.at[1 - core],
            send_sem=final_sem_tx.at[k],
            recv_sem=final_sem_rx.at[1 - core],
            device_id=edge_to[k],
            device_id_type=MESH,
        )
        for k in range(2)
    ]
    for copy in final_sends:
        copy.start()
    table = exact_dot(final_tx[...], g_to[...])
    gains = gain[...].reshape(1, C)
    shifts = shift[...].reshape(1, C)

    def norm(v, sib_clip):
        at = 2 if sib_clip else 0
        return (v.astype(F32) - table[at : at + 1]) * (table[at + 1 : at + 2] * gains) + shifts

    swap_pick.wait_recv()
    for g in range(3):
        part = slice(8 * g, 8 * g + 8)
        pair = jnp.concatenate([norm(pick_own[part], False), norm(pick_rx[part], True)], axis=0)
        ctx[g, 0:16, :] = pair.astype(BF16)

    def leaves_down(i, s):
        if i < 2:
            return edge_up if s == 0 else 1 - edge_down
        return s

    def hop(i, j, s):
        if j == 0:
            if i == 0:
                src, to = (0, 0, 0), y_pair
            elif i == 1:
                src, to = (0, 0, s), a_up
            elif i == 2:
                src, to = (0, 0, s), a_down
            else:
                src, to = ((1, 0, 0), a_up) if s == 0 else ((2, 0, 1), a_down)
        elif j == 1:
            src, to = (i, 0, s), b_up
        elif j == 2:
            src, to = (i, 0, s), b_down
        else:
            down = leaves_down(i, s)
            src, to = (i, 1 + down, s), along(False, 1 + 2 * down)
        n, dst = slot_of(*src), slot_of(i, j, s)
        return pltpu.make_async_remote_copy(
            src_ref=ctx.at[:, pl.ds(pl.multiple_of(16 * n, 16), 16), :],
            dst_ref=ctx.at[:, 16 * dst : 16 * dst + 16, :],
            send_sem=send_sem.at[dst],
            recv_sem=recv_sem.at[dst],
            device_id=to,
            device_id_type=MESH,
        )

    def start(*slots):
        for slot in slots:
            hop(*slot).start()

    start((0, 0, 1), (1, 0, 0), (2, 0, 0), (0, 1, 0), (0, 2, 0))

    def edge_arrived(n):
        pltpu.make_async_copy(edge_rx.at[n], edge_rx.at[n], misc_rx.at[3 + n]).wait()
        pltpu.make_async_copy(final_rx.at[n], final_rx.at[n], final_sem_rx.at[n]).wait()

    def pass_on(arrived, *slots):
        def act():
            hop(*arrived).wait_recv()
            start(*slots)

        return act

    def arrive(i, j, s):
        n = slot_of(i, j, s)
        here = ctx.at[:, pl.ds(pl.multiple_of(16 * n, 16), 16), :]
        pltpu.make_async_copy(here, here, recv_sem.at[n]).wait()

    def forward(i, s):
        def act():
            arrive(i, 1 + leaves_down(i, s), s)
            start((i, 3, s))

        return act

    def project(rows, m):
        return dot(rows, w[m])

    def kv_steps(rows, store, *acts):
        def step(m, _):
            for n, act in enumerate(acts):
                pl.when(m == n)(act)
            store(m, project(rows(), 1 + m))
            return 0

        lax.fori_loop(0, 2, step, 0)

    def store_rows(at, n):
        def store(m, res):
            kv[m, :, at : at + n, :] = res.astype(BF16).reshape(HALF, n, C)

        return store

    def gather_ctx(j, at):
        for g in range(3):
            rows = dot(s8[...], ctx[g, 128 * j : 128 * j + 128, :]).astype(BF16)
            xc[8 * g : 8 * g + 8, at : at + 16, :] = rows.reshape(8, 16, C)

    def many(*acts):
        def act():
            for one in acts:
                one()

        return act

    own_x[:, 0:16, :] = norm(turned[pl.ds(HALF * core, HALF)], False).astype(BF16)
    swap_rows.wait_recv()
    own_x[:, 16:32, :] = norm(sib[...], True).astype(BF16)

    def own_rows():
        return own_x[...].reshape(HALF * 32, C)

    loads[8].wait()
    query[...] = (project(own_rows(), 0) * (HEAD_DIM**-0.5)).astype(BF16).reshape(HALF, 32, C)
    loads[9].wait()
    loads[10].wait()
    kv_steps(
        own_rows,
        store_rows(64, 32),
        many(
            pass_on((0, 0, 1), (1, 0, 1), (2, 0, 1), (0, 1, 1), (0, 2, 1)),
            pass_on((1, 0, 0), (3, 0, 0), (1, 1, 0), (1, 2, 0)),
            pass_on((2, 0, 0), (2, 1, 0), (2, 2, 0)),
            send_edges,
            forward(0, 0),
        ),
        many(
            pass_on((2, 0, 1), (3, 0, 1), (2, 1, 1), (2, 2, 1)),
            pass_on((1, 0, 1), (1, 1, 1), (1, 2, 1)),
        ),
    )
    pass_on((3, 0, 0), (3, 1, 0), (3, 2, 0))()
    forward(0, 1)()
    pass_on((3, 0, 1), (3, 1, 1), (3, 2, 1))()
    loads[11].wait()
    gather_ctx(0, 0)

    def one_phase():
        return xc[:, 0:16, :].reshape(HALF * 16, C)

    kv_steps(one_phase, store_rows(0, 16), forward(1, 0), many(forward(2, 0), forward(2, 1)))

    forward(1, 1)()
    forward(3, 0)()
    forward(3, 1)()
    for i in range(4):
        for s in range(2):
            arrive(i, 2 - leaves_down(i, s), s)
    gather_ctx(1, 0)
    gather_ctx(2, 16)
    kv_steps(lambda: xc[...].reshape(HALF * 32, C), store_rows(16, 32))
    loads[12].wait()
    edge_arrived(0)
    edge_arrived(1)
    left_side = lax.broadcasted_iota(jnp.int32, (8, C), 0) < EDGE
    left_table = exact_dot(final_rx[0], g_to[...])
    right_table = exact_dot(final_rx[1], g_to[...])
    edge_mean = jnp.where(left_side, left_table[0:1], right_table[0:1])
    edge_gain = jnp.where(left_side, left_table[1:2] * gains, right_table[1:2] * gains)
    rows = dot(e_in[...], edge_rx[...].reshape(192, C)).reshape(HALF, 8, C)
    edge_x[...] = ((rows - edge_mean) * edge_gain + shifts).astype(BF16).reshape(HALF * 8, C)

    def edge_rows_in():
        return edge_x[...]

    def store_edges(m, res):
        res = jnp.concatenate([res.reshape(HALF, 8, C), jnp.zeros((HALF, 8, C), F32)], axis=1)
        kv[m, :, 96:112, :] = res.astype(BF16)

    kv_steps(edge_rows_in, store_edges)

    for i in range(4):
        for s in range(2):
            hop(i, 3, s).wait_recv()
    gather_ctx(3, 0)
    kv_steps(one_phase, store_rows(48, 16))

    loads[13].wait()
    loads[14].wait()

    def send_att(c):
        there = pl.ds(HALF * core + 8 * c, 8)
        return pltpu.make_async_remote_copy(
            src_ref=att_tx.at[8 * c : 8 * c + 8],
            dst_ref=att.at[there],
            send_sem=att_sem_tx.at[c],
            recv_sem=att_sem_rx.at[c],
            device_id=sibling,
            device_id_type=MESH,
        )

    def attend(block, _):
        half = lax.broadcasted_iota(jnp.int32, (32, 128), 1) < HEAD_DIM
        units = [(block * 4 + n, h) for n in range(4) for h in range(TILES)]
        cols = [slice(h * TILE, (h + 1) * TILE) for h in range(TILES)]
        scores, weights, mixed = [], [], []
        for p, h in units:
            q = jnp.concatenate([query[p, :, cols[h]]] * 4, axis=0) * h_mask[...]
            scores.append(
                lax.dot_general(kv[0, p, :, cols[h]], q, (((1,), (1,)), ((), ())), preferred_element_type=F32)
            )
        for s in scores:
            s = jnp.concatenate([s[:64], s[64:] + mask[...]], axis=0)
            expo = jnp.exp(s - jnp.max(s, axis=0, keepdims=True))
            share = 1.0 / jnp.sum(expo, axis=0, keepdims=True)
            weights.append((expo * share).astype(BF16))
        for (p, h), s in zip(units, weights):
            mixed.append(
                lax.dot_general(s, kv[1, p, :, cols[h]], (((0,), (0,)), ((), ())), preferred_element_type=F32)
            )
        for (p, h), m in zip(units, mixed):
            for t in range(2):
                lanes = slice(128 * t, 128 * t + 128)
                both = jnp.where(half, m[64 * t : 64 * t + 32, lanes], m[64 * t + 32 : 64 * t + 64, lanes])
                both = both.astype(BF16)
                to = slice(h * TILE + 128 * t, h * TILE + 128 * t + 128)
                att[HALF * core + p, :, to] = both[:16]
                att_tx[p, :, to] = both[16:]
        return 0

    for c in range(3):
        lax.fori_loop(2 * c, 2 * c + 2, attend, 0)
        send_att(c).start()

    def att_arrived(c):
        there = pl.ds(HALF * (1 - core) + 8 * c, 8)
        pltpu.make_async_copy(att.at[there], att.at[there], att_sem_rx.at[c]).wait()

    loads[7].wait()

    stores = []
    for t in range(3):
        if t == 1:
            att_arrived(0)
            att_arrived(1)
        elif t == 2:
            att_arrived(2)
        q = (t + 2 * core) % 3
        there = pl.ds(pl.multiple_of(q * 16, 16), 16)
        rows = dot(s16[...], att[there].reshape(256, C)).astype(BF16)
        res = dot(rows, w_out[...]).reshape(FRAMES, 16, C) + out_bias[...].reshape(1, 1, C)
        result[t] = (lat[:, there, :].astype(F32) + res).astype(BF16)
        stores.append(pltpu.make_async_copy(result.at[t], out.at[:, there, :], store_sem.at[t]))
        stores[t].start()

    for copy in stats:
        copy.wait_send()
    swap_pick.wait_send()
    swap_rows.wait_send()
    for copy in final_sends + [passing]:
        copy.wait_send()

    @pl.when(core == y)
    def _():
        for copy in relays:
            copy.wait_send()

    @pl.when(core != y)
    def _():
        for copy in directs:
            copy.wait_send()

    for j in range(4):
        for i in range(4):
            for s in range(2):
                if (i, j, s) != (0, 0, 0):
                    hop(i, j, s).wait_send()
    for c in range(3):
        send_att(c).wait_send()
    for copy in stores:
        copy.wait()


def local(latent, gn_gain, gn_bias, w_query, w_key, w_value, w_out, out_bias, context_frames):
    consts = [
        jnp.asarray(SWAP16, BF16),
        jnp.asarray(SWAP8, BF16),
        jnp.asarray(EDGE_OUT, BF16),
        jnp.asarray(EDGE_IN, BF16),
        jnp.asarray(GROUP_OF, BF16),
        jnp.asarray(GROUP_OF.T.copy(), BF16),
        jnp.asarray(HEAD_MASK, BF16),
    ]
    any_ = pl.BlockSpec(memory_space=pl.ANY)
    smem = pl.BlockSpec(memory_space=pltpu.SMEM)
    dma = pltpu.SemaphoreType.DMA
    return pl.pallas_call(
        kernel,
        out_shape=jax.ShapeDtypeStruct((FRAMES, ROWS, C), BF16),
        in_specs=[any_] * 8 + [smem] + [any_] * 7,
        out_specs=any_,
        scratch_shapes=[
            pltpu.VMEM((FRAMES, ROWS, C), BF16),
            pltpu.VMEM((ROWS, FRAMES, C), BF16),
            pltpu.VMEM((HALF, FRAMES, C), BF16),
            pltpu.VMEM((HALF, 32, C), BF16),
            pltpu.VMEM((3, 512, C), BF16),
            pltpu.VMEM((HALF, 32, C), BF16),
            pltpu.VMEM((2, 96, C), BF16),
            pltpu.VMEM((96, C), BF16),
            pltpu.VMEM((2, 96, C), BF16),
            pltpu.VMEM((192, C), BF16),
            pltpu.VMEM((HALF, 32, C), BF16),
            pltpu.VMEM((2, HALF, KEYS, C), BF16),
            pltpu.VMEM((ROWS, FRAMES, C), BF16),
            pltpu.VMEM((HALF, FRAMES, C), BF16),
            pltpu.VMEM((3, FRAMES, 16, C), BF16),
            pltpu.VMEM((3, C, C), BF16),
            pltpu.VMEM((C, C), BF16),
            pltpu.VMEM((256, 256), BF16),
            pltpu.VMEM((128, 128), BF16),
            pltpu.VMEM((192, 192), BF16),
            pltpu.VMEM((192, 192), BF16),
            pltpu.VMEM((C, 128), BF16),
            pltpu.VMEM((128, C), BF16),
            pltpu.VMEM((128, TILE), BF16),
            pltpu.VMEM((C,), F32),
            pltpu.VMEM((C,), F32),
            pltpu.VMEM((C,), F32),
            pltpu.VMEM((8, 128), F32),
            pltpu.VMEM((3, 8, 128), F32),
            pltpu.VMEM((8, 128), F32),
            pltpu.VMEM((2, 8, 128), F32),
            pltpu.VMEM((HALF, C), F32),
            pltpu.VMEM((HALF, C), F32),
            pltpu.VMEM((HALF, C), F32),
            pltpu.VMEM((48, 128), F32),
            dma((15,)),
            dma((32,)),
            dma((32,)),
            dma((8,)),
            dma((5,)),
            dma((3,)),
            dma((3,)),
            dma((2,)),
            dma((2,)),
            dma,
            dma((3,)),
            dma((3,)),
            dma((3,)),
        ],
        compiler_params=pltpu.CompilerParams(
            collective_id=0, has_side_effects=True, vmem_limit_bytes=60 * 1024 * 1024
        ),
        cost_estimate=pl.CostEstimate(flops=25 * 10**9, bytes_accessed=18 * 10**6, transcendentals=2 * 10**6),
    )(
        latent, gn_gain, gn_bias, w_query, w_key, w_value, w_out,
        out_bias, context_frames, *consts,
    )


def solution(mesh):
    placed = (P("clip", "space", None), P(), P(), P(), P(), P(), P(), P(), P("clip", None))
    return jax.shard_map(
        local, mesh=mesh, in_specs=placed, out_specs=P("clip", "space", None), check_vma=False
    )
```

time: 68.5 us -> 61.3 us (0.89)
  the two profiles are of different devices: /device:TPU:5 before, /device:TPU:9 now
where the time goes in v3:
time: 61.3 us; the launch traced here: 61.1 us
  Pallas kernels  57.5 us (94%)
  local copies, waits for them, and re-layouts  2.94 us (5%)
  between operations  0.66 us (1%)
    pallas_call x1, Pallas kernels, local(): pl.pallas_call(kernel, out_shape=jax.ShapeDtypeStruct((FRAMES, ROWS, C),...  57.5 us
    unnamed x1, local copies, waits for them, and re-layouts  2.94 us

profile of v3, /device:TPU:9, one launch (start us, length us, event | category | flops | bytes accessed | tf_op | source)
XLA Modules:
  0.0 61.1 jit_solution(4739062521062888359)
XLA Ops:
  0.7 57.5 %shard_map.154 = bf16[16,48,1280]{2,1,0:T(8,128)(2,1)} custom-call(bf16[16,48,1280]{2,1,0:T(8,128)(2,1)} %latent.1, f32[1280]{0:T(1024)} %gain_in.1, f32[1280]{0:T(1024)} %shift_in.1, bf16[1280,1280]{1,0:T(8,128)(2,1)} %wq.1, bf16[1280,1280]{1,0:T(8,128)(2,1)} %wk.1, bf16[1280,1280]{1,0:T(8,128)(2,1)} %wv.1, bf16[1280,1280]{1,0:T(8,128)(2,1)} %wo.1, ...), custom_call_target="tpu_custom_call" | custom-call | flops 24999999488 | bytes 18000000 | tf_op jit(solution)/shard_map/pallas_call | solution.py:586
  58.2 2.9 %copy.19 = bf16[16,48,1280]{2,1,0:T(8,128)(2,1)} copy(bf16[16,48,1280]{2,1,0:T(8,128)(2,1)} %shard_map.154) | data formatting | bytes 3932160

commit v4 on v3

--- a/solution.py
+++ b/solution.py
@@ -71,7 +71,7 @@
 def kernel(
     latent, gain_in, shift_in, wq, wk, wv, wo, bias_in, picks, swap16, swap8, edge_out, edge_in, group_of, group_to, head_mask,
     out,
-    lat, turned, sib, own_x, ctx, xc, edge_tx, edge_relay, edge_rx, edge_x, query, kv, att, att_tx, result, w, w_out,
+    lat, turned, sib, own_x, ctx, xc, edge_tx, edge_relay, edge_cross, edge_rx, edge_x, query, kv, att, att_tx, result, w, w_out,
     s16, s8, e_out, e_in, g_of, g_to, h_mask, gain, shift, out_bias, stat_tx, stat_rx, final_tx, final_rx, pick_own, pick_tx, pick_rx, mask,
     load_sem, send_sem, recv_sem, misc_tx, misc_rx, stat_sem_tx, stat_sem_rx, final_sem_tx, final_sem_rx, relay_rx, att_sem_tx, att_sem_rx, store_sem,
 ):
@@ -103,17 +103,16 @@
     relay_to = [device(x, relay_z, y, k) for k in range(2)]
     origin_z = (z + 5 - 2 * y) % 4
     relay_from = [device(x, origin_z, y, k) for k in range(2)]
-    pass_chip = ((x * 4 + origin_z) * 2 + y + 2 * y + 31) % 32
-    pass_to = (pass_chip * 2 + core, space)
-    near = (chip + 2 * y + 31) % 32
-    pass_from = device(near // 8, ((near // 2) % 4 + 2 * (1 - y) + 3) % 4, 1 - y, core)
+    crossing = y * (1 - (z + 2) // 3) + (1 - y) * (z // 3)
+    cross_to = device((x + 2 * y + 3) % 4, z, y, core)
+    cross_from = device((x + 5 - 2 * y) % 4, z, y, core)
 
     edge_up = core * y * (1 - (z + 2) // 3)
     edge_down = core * (1 - y) * (z // 3)
 
     barrier = pltpu.get_barrier_semaphore()
     greet = [a_up, a_down, b_up, b_down, y_pair] + stats_to + edge_to + edge_from
-    greet += relay_to + relay_from + [pass_to, pass_from]
+    greet += relay_to + relay_from + [cross_to, cross_from]
     for other in greet:
         pl.semaphore_signal(barrier, inc=1, device_id=other, device_id_type=MESH)
 
@@ -223,7 +222,7 @@
             src_ref=edge_tx.at[k],
             dst_ref=edge_relay,
             send_sem=misc_tx.at[3 + k],
-            recv_sem=relay_rx,
+            recv_sem=relay_rx.at[0],
             device_id=relay_to[k],
             device_id_type=MESH,
         )
@@ -240,14 +239,24 @@
         )
         for k in range(2)
     ]
-    passing = pltpu.make_async_remote_copy(
+    cross = pltpu.make_async_remote_copy(
         src_ref=edge_relay,
-        dst_ref=edge_rx.at[1 - y],
-        send_sem=misc_tx.at[7],
-        recv_sem=misc_rx.at[3 + 1 - y],
-        device_id=pass_to,
+        dst_ref=edge_cross,
+        send_sem=misc_tx.at[8],
+        recv_sem=relay_rx.at[1],
+        device_id=cross_to,
         device_id_type=MESH,
     )
+
+    def pass_along_y(src):
+        return pltpu.make_async_remote_copy(
+            src_ref=src,
+            dst_ref=edge_rx.at[1 - y],
+            send_sem=misc_tx.at[7],
+            recv_sem=misc_rx.at[3 + 1 - y],
+            device_id=y_pair,
+            device_id_type=MESH,
+        )
 
     @pl.when(core == y)
     def _():
@@ -260,8 +269,15 @@
             for copy in directs:
                 copy.start()
 
-        relays[0].wait_recv()
-        passing.start()
+        @pl.when(crossing == 0)
+        def _():
+            pass_along_y(edge_relay).start()
+
+    def send_crossed():
+        @pl.when(crossing == 1)
+        def _():
+            cross.wait_recv()
+            pass_along_y(edge_cross).start()
 
     loads[3].wait()
     for q in range(3):
@@ -406,6 +422,12 @@
     swap_rows.wait_recv()
     own_x[:, 16:32, :] = norm(sib[...], True).astype(BF16)
 
+    relays[0].wait_recv()
+
+    @pl.when(crossing == 1)
+    def _():
+        cross.start()
+
     def own_rows():
         return own_x[...].reshape(HALF * 32, C)
 
@@ -437,7 +459,7 @@
     def one_phase():
         return xc[:, 0:16, :].reshape(HALF * 16, C)
 
-    kv_steps(one_phase, store_rows(0, 16), forward(1, 0), many(forward(2, 0), forward(2, 1)))
+    kv_steps(one_phase, store_rows(0, 16), many(forward(1, 0), send_crossed), many(forward(2, 0), forward(2, 1)))
 
     forward(1, 1)()
     forward(3, 0)()
@@ -490,7 +512,7 @@
 
     def attend(block, _):
         half = lax.broadcasted_iota(jnp.int32, (32, 128), 1) < HEAD_DIM
-        units = [(block * 4 + n, h) for n in range(4) for h in range(TILES)]
+        units = [(block * 8 + n, h) for n in range(8) for h in range(TILES)]
         cols = [slice(h * TILE, (h + 1) * TILE) for h in range(TILES)]
         scores, weights, mixed = [], [], []
         for p, h in units:
@@ -518,7 +540,7 @@
         return 0
 
     for c in range(3):
-        lax.fori_loop(2 * c, 2 * c + 2, attend, 0)
+        lax.fori_loop(c, c + 1, attend, 0)
         send_att(c).start()
 
     def att_arrived(c):
@@ -546,8 +568,12 @@
         copy.wait_send()
     swap_pick.wait_send()
     swap_rows.wait_send()
-    for copy in final_sends + [passing]:
+    for copy in final_sends + [pass_along_y(edge_relay)]:
         copy.wait_send()
+
+    @pl.when(crossing == 1)
+    def _():
+        cross.wait_send()
 
     @pl.when(core == y)
     def _():
@@ -596,6 +622,7 @@
             pltpu.VMEM((3, 512, C), BF16),
             pltpu.VMEM((HALF, 32, C), BF16),
             pltpu.VMEM((2, 96, C), BF16),
+            pltpu.VMEM((96, C), BF16),
             pltpu.VMEM((96, C), BF16),
             pltpu.VMEM((2, 96, C), BF16),
             pltpu.VMEM((192, C), BF16),
@@ -627,13 +654,13 @@
             dma((15,)),
             dma((32,)),
             dma((32,)),
-            dma((8,)),
+            dma((9,)),
             dma((5,)),
             dma((3,)),
             dma((3,)),
             dma((2,)),
             dma((2,)),
-            dma,
+            dma((2,)),
             dma((3,)),
             dma((3,)),
             dma((3,)),

time: 61.3 us -> 59.8 us (0.976)
  the two profiles are of different devices: /device:TPU:9 before, /device:TPU:1 now
where the time goes in v4:
time: 59.8 us; the launch traced here: 59.7 us
  Pallas kernels  56.1 us (94%)
  local copies, waits for them, and re-layouts  2.94 us (5%)
  between operations  0.66 us (1%)
    pallas_call x1, Pallas kernels, local(): pl.pallas_call(kernel, out_shape=jax.ShapeDtypeStruct((FRAMES, ROWS, C),...  56.1 us
    unnamed x1, local copies, waits for them, and re-layouts  2.94 us

profile of v4, /device:TPU:1, one launch (start us, length us, event | category | flops | bytes accessed | tf_op | source)
XLA Modules:
  0.0 59.7 jit_solution(11994415817377315015)
XLA Ops:
  0.7 56.1 %shard_map.154 = bf16[16,48,1280]{2,1,0:T(8,128)(2,1)} custom-call(bf16[16,48,1280]{2,1,0:T(8,128)(2,1)} %latent.1, f32[1280]{0:T(1024)} %gain_in.1, f32[1280]{0:T(1024)} %shift_in.1, bf16[1280,1280]{1,0:T(8,128)(2,1)} %wq.1, bf16[1280,1280]{1,0:T(8,128)(2,1)} %wk.1, bf16[1280,1280]{1,0:T(8,128)(2,1)} %wv.1, bf16[1280,1280]{1,0:T(8,128)(2,1)} %wo.1, ...), custom_call_target="tpu_custom_call" | custom-call | flops 24999999488 | bytes 18000000 | tf_op jit(solution)/shard_map/pallas_call | solution.py:612
  56.7 2.9 %copy.19 = bf16[16,48,1280]{2,1,0:T(8,128)(2,1)} copy(bf16[16,48,1280]{2,1,0:T(8,128)(2,1)} %shard_map.154) | data formatting | bytes 3932160

commit v5 on v4

--- a/solution.py
+++ b/solution.py
@@ -159,29 +159,28 @@
     for copy in loads[8:]:
         copy.start()
 
-    def add_rows(f, acc):
-        v = lat[f].astype(F32)
-        for r in range(ROWS // 8):
+    def fold(v):
+        acc = v[:8]
+        for r in range(1, ROWS // 8):
             acc = acc + v[8 * r : 8 * r + 8]
         return acc
 
-    total = lax.fori_loop(0, FRAMES, add_rows, jnp.zeros((8, C), F32))
     loads[1].wait()
     loads[2].wait()
     count = FRAMES * ROWS * (C // GROUPS)
-    mean_here = jnp.sum(exact_dot(total, g_of[...]), axis=0, keepdims=True) * (1.0 / count)
-    mean_here = jnp.broadcast_to(mean_here, (8, 128))
-    wide = exact_dot(mean_here, g_to[...])
-
-    def add_squares(f, acc):
-        v = lat[f].astype(F32)
-        for r in range(ROWS // 8):
-            d = v[8 * r : 8 * r + 8] - wide
-            acc = acc + d * d
-        return acc
-
-    squares = lax.fori_loop(0, FRAMES, add_squares, jnp.zeros((8, C), F32))
-    dev_here = jnp.sum(exact_dot(squares, g_of[...]), axis=0, keepdims=True)
+    about = jnp.sum(exact_dot(fold(lat[0].astype(F32)), g_of[...]), axis=0, keepdims=True) * (FRAMES / count)
+    wide = exact_dot(jnp.broadcast_to(about, (8, 128)), g_to[...])[0:1]
+
+    def add_frame(f, acc):
+        d = lat[f].astype(F32) - wide
+        return acc[0] + fold(d), acc[1] + fold(d * d)
+
+    zero = jnp.zeros((8, C), F32)
+    sums = exact_dot(jnp.concatenate(lax.fori_loop(0, FRAMES, add_frame, (zero, zero)), axis=0), g_of[...])
+    shift_sum = jnp.sum(sums[:8], axis=0, keepdims=True)
+    square_sum = jnp.sum(sums[8:], axis=0, keepdims=True)
+    mean_here = jnp.broadcast_to(about + shift_sum * (1.0 / count), (8, 128))
+    dev_here = jnp.maximum(square_sum - shift_sum * shift_sum * (1.0 / count), 0.0)
     dev_here = jnp.broadcast_to(dev_here, (8, 128))
     first_row = lax.broadcasted_iota(jnp.int32, (8, 128), 0) == 0
     stat_tx[...] = jnp.where(first_row, mean_here, dev_here)

time: 59.8 us -> 59.8 us (level)
  no operation moved by 1% of the time
where the time goes in v5:
time: 59.8 us; the launch traced here: 59.7 us
  Pallas kernels  56.1 us (94%)
  local copies, waits for them, and re-layouts  2.94 us (5%)
  between operations  0.66 us (1%)
    pallas_call x1, Pallas kernels, local(): pl.pallas_call(kernel, out_shape=jax.ShapeDtypeStruct((FRAMES, ROWS, C),...  56.1 us
    unnamed x1, local copies, waits for them, and re-layouts  2.94 us

profile of v5, /device:TPU:1, one launch (start us, length us, event | category | flops | bytes accessed | tf_op | source)
XLA Modules:
  0.0 59.7 jit_solution(11827523320916119573)
XLA Ops:
  0.7 56.1 %shard_map.154 = bf16[16,48,1280]{2,1,0:T(8,128)(2,1)} custom-call(bf16[16,48,1280]{2,1,0:T(8,128)(2,1)} %latent.1, f32[1280]{0:T(1024)} %gain_in.1, f32[1280]{0:T(1024)} %shift_in.1, bf16[1280,1280]{1,0:T(8,128)(2,1)} %wq.1, bf16[1280,1280]{1,0:T(8,128)(2,1)} %wk.1, bf16[1280,1280]{1,0:T(8,128)(2,1)} %wv.1, bf16[1280,1280]{1,0:T(8,128)(2,1)} %wo.1, ...), custom_call_target="tpu_custom_call" | custom-call | flops 24999999488 | bytes 18000000 | tf_op jit(solution)/shard_map/pallas_call | solution.py:611
  56.7 2.9 %copy.19 = bf16[16,48,1280]{2,1,0:T(8,128)(2,1)} copy(bf16[16,48,1280]{2,1,0:T(8,128)(2,1)} %shard_map.154) | data formatting | bytes 3932160
